TPU v7x, 256 devices: a whole 4x4x8 slice. The times are simulated.
256 devices in a mesh: rows: 32 (over x, z_lo, core), cols: 8 (over z_hi, y).
Axes of the slice: x: 4, y: 4, z: 8 (z_hi: 2, z_lo: 4; z = z_hi * 4 + z_lo), core: 2. Of those that a mesh axis runs over, the one named last changes fastest.
Arguments:
- row_factor: bfloat16 [65536, 512], P(('rows', 'cols')), may hold values from -1.1953125 to 1.1953125
- col_factor: bfloat16 [262144, 512], P(('rows', 'cols')), may hold values from -1.1953125 to 1.1953125
- tiles: bfloat16 [2, 32, 8, 16, 256, 256], P(None, 'rows', 'cols'), may hold values from -6 to 6
- tile_rows: int32 [2, 32, 8, 16], P(None, 'rows', 'cols'), may hold values from 0 to 7, as said below
- tile_cols: int32 [2, 32, 8, 16], P(None, 'rows', 'cols'), may hold values from 0 to 3, as said below
- tile_counts: int32 [2, 32, 8], P(None, 'rows', 'cols'), may hold values from 2 to 16, as said below
- matching: int32 [2, 32], replicated, may hold values from 0 to 31, as said below
- row_noise: bfloat16 [2, 65536, 512], P(None, ('rows', 'cols')), may hold values from -6 to 6
- col_noise: bfloat16 [2, 262144, 512], P(None, ('rows', 'cols')), may hold values from -6 to 6
- step_sizes: float32 [2], replicated, may hold values from 0.01 to 0.04
Outputs:
- row_sample: bfloat16 [65536, 512], P(('rows', 'cols'))
- col_sample: bfloat16 [262144, 512], P(('rows', 'cols'))
Inputs may be any that keep to these rules, and one draw needn't show every extreme that they name: In each stratum, row block and panel, the 16 slots name distinct tile positions (tile_rows, tile_cols) among 8 x 4. `tile_cols`: see tile_rows. `tile_counts`: in each stratum some row block and panel have exactly 16 observed tiles; slots from the count on hold tiles that are not observed. matching[s, b] is b bitwise exclusive or matching[s, 0]; matching[1, b] is matching[0, b] bitwise exclusive or (31).
All inputs are finite; a program needn't handle non-finite values.
Results may differ from a plain program's by a relative error of at most 0.02.
Values may be sent and summed in bfloat16 or wider, within the bound.
No kernel may reach another device: no remote copies, remote signals or barrier semaphores. Data moves between devices by JAX's collectives and lax.ppermute only.
A program may use at most 64 MiB of HBM per device.

v0:
```python
import functools

import jax
import jax.numpy as jnp
from jax import lax
from jax.experimental import pallas as pl
from jax.experimental.pallas import tpu as pltpu
from jax.sharding import PartitionSpec as P

TILE = 256
PEERS = 8
GROUP = 4

prior_precision = 1.0


def swap(value, axis, mask):
    return lax.ppermute(value, axis, [(i, i ^ mask) for i in range(lax.axis_size(axis))])


def langevin(current, gradient, gaussian, step_size):
    current_wide = current.astype(jnp.float32)
    return (
        current_wide
        + 0.5 * step_size * (gradient - prior_precision * current_wide)
        + jnp.sqrt(step_size) * gaussian.astype(jnp.float32)
    )


def wide(value):
    return value.astype(jnp.float32)


def after(value, *others):
    return lax.optimization_barrier((value,) + others)[0]


def swap_near(parts, base):
    pick = (lambda k: parts[base + k]) if isinstance(parts, (list, tuple)) else (lambda k: parts)
    return [swap(pick(k), "cols", k) for k in (1, 2, 3)]


def stratum_kernel(stratum, me, step, row_pick, col_pick, count, *refs):
    u_in, (va_in, vb_in, tiles, noise) = refs[:PEERS], refs[PEERS : PEERS + 4]
    q_out, (va_out, vb_out) = refs[PEERS + 4 : 2 * PEERS + 4], refs[2 * PEERS + 4 : 2 * PEERS + 6]
    u_s, v_s, t_s, n_s, r_acc, c_acc, q_s, u_sem, v_sem, t_sem, n_sem, o_sem = refs[2 * PEERS + 6 :]
    n_group = t_s.shape[0] // GROUP
    cut = va_in.shape[0]
    spans = (pl.ds(0, cut), pl.ds(cut, v_s.shape[0] - cut))
    loads = [pltpu.make_async_copy(u_in[k], u_s.at[k], u_sem.at[k]) for k in range(PEERS)]
    for i, v_in in enumerate((va_in, vb_in)):
        loads.append(pltpu.make_async_copy(v_in, v_s.at[spans[i]], v_sem.at[i]))

    def tile_load(i):
        span = pl.ds(i * GROUP, GROUP)
        return pltpu.make_async_copy(tiles.at[stratum, 0, 0, span], t_s.at[span], t_sem.at[i])

    noise_load = pltpu.make_async_copy(noise.at[stratum], n_s, n_sem.at[0])
    for copy in loads:
        copy.start()
    for i in range(n_group):
        tile_load(i).start()
    noise_load.start()
    r_acc[...] = jnp.zeros_like(r_acc)
    c_acc[...] = jnp.zeros_like(c_acc)
    for copy in loads:
        copy.wait()
    total = count[stratum, 0, 0]

    def group(i, carry):
        tile_load(i).wait()
        work = []
        for j in range(GROUP):
            t = i * GROUP + j
            r = row_pick[stratum, 0, 0, t] ^ me[0]
            c = pl.ds(pl.multiple_of(col_pick[stratum, 0, 0, t] * TILE, TILE), TILE)
            predicted = lax.dot_general(
                u_s[r], v_s[c], (((1,), (1,)), ((), ())), preferred_element_type=jnp.float32
            )
            residual = (wide(t_s[t]) - predicted).astype(jnp.bfloat16)
            work.append((r, c, jnp.where(t < total, residual, jnp.zeros_like(residual))))
        for r, c, residual in work:
            r_acc[r] += jnp.dot(residual, v_s[c], preferred_element_type=jnp.float32)
            c_acc[c] += lax.dot_general(
                residual, u_s[r], (((0,), (0,)), ((), ())), preferred_element_type=jnp.float32
            )
        return carry

    def unused(i, carry):
        tile_load(i).wait()
        return carry

    used = (total + GROUP - 1) // GROUP
    lax.fori_loop(0, used, group, 0)
    lax.fori_loop(used, n_group, unused, 0)
    stores = []
    for k in (5, 6, 7, 4, 1, 2, 3, 0):
        q_s[k] = r_acc[k].astype(jnp.bfloat16)
        stores.append(pltpu.make_async_copy(q_s.at[k], q_out[k], o_sem.at[k]))
        stores[-1].start()
    h = step[stratum]
    root = jnp.sqrt(jnp.full((1, 1), h, jnp.float32))
    noise_load.wait()
    for i, v_out in enumerate((va_out, vb_out)):
        for low in range(spans[i].start, spans[i].start + spans[i].size, TILE // 2):
            rows = pl.ds(low, TILE // 2)
            current = wide(v_s[rows])
            moved = (
                current
                + (0.5 * h) * (c_acc[rows] - prior_precision * current)
                + root * wide(n_s[rows])
            )
            v_s[rows] = moved.astype(jnp.bfloat16)
        stores.append(pltpu.make_async_copy(v_s.at[spans[i]], v_out, o_sem.at[PEERS + i]))
        stores[-1].start()
    for copy in stores:
        copy.wait()


def stratum_step(stratum, me, step_sizes, tile_rows, tile_cols, tile_counts, rows, halves, tiles, noise):
    n_col, rank = noise.shape[1:]
    n_slot = tiles.shape[3]
    smem = pl.BlockSpec(memory_space=pltpu.SMEM)
    free = pl.BlockSpec(memory_space=pl.ANY)
    part = jax.ShapeDtypeStruct((TILE, rank), jnp.bfloat16)
    out = pl.pallas_call(
        functools.partial(stratum_kernel, stratum),
        out_shape=[part] * PEERS
        + [jax.ShapeDtypeStruct(v.shape, jnp.bfloat16) for v in halves],
        in_specs=[smem] * 5 + [free] * (PEERS + 4),
        out_specs=[free] * (PEERS + 2),
        scratch_shapes=[
            pltpu.VMEM((PEERS, TILE, rank), jnp.bfloat16),
            pltpu.VMEM((n_col, rank), jnp.bfloat16),
            pltpu.VMEM((n_slot, TILE, TILE), jnp.bfloat16),
            pltpu.VMEM((n_col, rank), jnp.bfloat16),
            pltpu.VMEM((PEERS, TILE, rank), jnp.float32),
            pltpu.VMEM((n_col, rank), jnp.float32),
            pltpu.VMEM((PEERS, TILE, rank), jnp.bfloat16),
            pltpu.SemaphoreType.DMA((PEERS,)),
            pltpu.SemaphoreType.DMA((2,)),
            pltpu.SemaphoreType.DMA((n_slot // GROUP,)),
            pltpu.SemaphoreType.DMA((1,)),
            pltpu.SemaphoreType.DMA((PEERS + 2,)),
        ],
        compiler_params=pltpu.CompilerParams(vmem_limit_bytes=46 * 1024 * 1024),
        cost_estimate=pl.CostEstimate(
            flops=6 * n_slot * TILE * TILE * rank, bytes_accessed=9 << 20, transcendentals=0
        ),
        name="stratum_%d" % stratum,
    )(me, step_sizes, tile_rows, tile_cols, tile_counts, *rows, *halves, tiles, noise)
    return out[:PEERS], out[PEERS:]


def finish_kernel(step, *refs):
    part_in, (shard, noise, va_in, vb_in) = refs[:5], refs[5:9]
    row_out, col_out, part_s, own_s, sem, col_sem = refs[9:]
    stratum = noise.shape[0] - 1
    cut = va_in.shape[0]
    copies = [
        pltpu.make_async_copy(va_in, col_out.at[pl.ds(0, cut)], col_sem.at[0]),
        pltpu.make_async_copy(
            vb_in, col_out.at[pl.ds(cut, vb_in.shape[0])], col_sem.at[1]
        ),
    ]
    loads = [pltpu.make_async_copy(part_in[i], part_s.at[i], sem.at[i]) for i in range(5)]
    loads.append(pltpu.make_async_copy(shard, own_s.at[0], sem.at[5]))
    loads.append(pltpu.make_async_copy(noise.at[stratum], own_s.at[1], sem.at[6]))
    for copy in copies + loads:
        copy.start()
    for copy in loads:
        copy.wait()
    total = wide(part_s[0]) + wide(part_s[1]) + wide(part_s[2]) + wide(part_s[3]) + wide(part_s[4])
    h = step[stratum]
    root = jnp.sqrt(jnp.full((1, 1), h, jnp.float32))
    current = wide(own_s[0])
    moved = current + (0.5 * h) * (total - prior_precision * current) + root * wide(own_s[1])
    row_out[...] = moved.astype(jnp.bfloat16)
    for copy in copies:
        copy.wait()


def finish(step_sizes, terms, shard, row_noise, upper, lower):
    free = pl.BlockSpec(memory_space=pl.ANY)
    panel = (upper.shape[0] + lower.shape[0], upper.shape[1])
    return pl.pallas_call(
        finish_kernel,
        out_shape=[
            jax.ShapeDtypeStruct(shard.shape, jnp.bfloat16),
            jax.ShapeDtypeStruct(panel, jnp.bfloat16),
        ],
        in_specs=[pl.BlockSpec(memory_space=pltpu.SMEM)] + [free] * 9,
        out_specs=[pl.BlockSpec(memory_space=pltpu.VMEM), free],
        scratch_shapes=[
            pltpu.VMEM((5,) + shard.shape, jnp.bfloat16),
            pltpu.VMEM((2,) + shard.shape, jnp.bfloat16),
            pltpu.SemaphoreType.DMA((7,)),
            pltpu.SemaphoreType.DMA((2,)),
        ],
        compiler_params=pltpu.CompilerParams(vmem_limit_bytes=16 * 1024 * 1024),
        name="finish",
    )(step_sizes, *terms, shard, row_noise, upper, lower)


def on_device(
    row_factor,
    col_factor,
    tiles,
    tile_rows,
    tile_cols,
    tile_counts,
    matching,
    row_noise,
    col_noise,
    step_sizes,
):
    me = lax.axis_index("cols").astype(jnp.int32).reshape(1)
    blocks = lax.axis_size("rows")
    first = matching[0, 0]
    cut = col_factor.shape[0] * 3 // 8

    def enter(mask, span, panel):
        piece = panel[span]
        return swap(piece, "rows", mask) if mask else piece

    def leave(mask, piece):
        return swap(piece, "rows", mask) if mask else piece

    def route(branch, flip, *operands):
        return lax.switch(
            first, [functools.partial(branch, k ^ flip) for k in range(blocks)], *operands
        )

    def kernel(stratum, rows, halves):
        return stratum_step(
            stratum, me, step_sizes, tile_rows, tile_cols, tile_counts, rows, halves, tiles, col_noise
        )

    partner = swap(row_factor, "cols", 4)
    near = swap_near(row_factor, 0)
    upper = route(lambda k, v: enter(k, slice(0, cut), v), 0, col_factor)
    partner, upper, near = lax.optimization_barrier((partner, upper, near))
    far = swap_near(partner, 0)
    lower = route(lambda k, v: enter(k, slice(cut, None), v), 0, after(col_factor, partner))
    parts, halves = kernel(0, [row_factor] + near + [partner] + far, (upper, lower))

    far = swap_near(parts, 4)
    upper = swap(halves[0], "rows", blocks - 1)
    near = swap_near(parts, 0)
    far_sum = wide(parts[4]) + wide(far[0]) + wide(far[1]) + wide(far[2])
    partner = swap(far_sum.astype(jnp.bfloat16), "cols", 4)
    partner, upper = lax.optimization_barrier((partner, upper))
    total = wide(parts[0]) + wide(near[0]) + wide(near[1]) + wide(near[2]) + wide(partner)
    shard = langevin(row_factor, total, row_noise[0], step_sizes[0]).astype(jnp.bfloat16)

    partner = swap(shard, "cols", 4)
    near = swap_near(shard, 0)
    partner, near = lax.optimization_barrier((partner, near))
    far = swap_near(partner, 0)
    lower = swap(after(halves[1], partner), "rows", blocks - 1)
    parts, halves = kernel(1, [shard] + near + [partner] + far, (upper, lower))

    far = swap_near(parts, 4)
    upper = route(leave, blocks - 1, halves[0])
    far_sum = wide(parts[4]) + wide(far[0]) + wide(far[1]) + wide(far[2])
    far_sum, upper = lax.optimization_barrier((far_sum.astype(jnp.bfloat16), upper))
    partner = swap(far_sum, "cols", 4)
    near = swap_near([after(part, far_sum) for part in parts[:4]], 0)
    lower = route(leave, blocks - 1, after(halves[1], far_sum))
    return finish(step_sizes, [parts[0]] + near + [partner], shard, row_noise, upper, lower)


def solution(mesh):
    return jax.shard_map(
        on_device,
        mesh=mesh,
        in_specs=(
            P(("rows", "cols"), None),
            P(("rows", "cols"), None),
            P(None, "rows", "cols", None, None, None),
            P(None, "rows", "cols", None),
            P(None, "rows", "cols", None),
            P(None, "rows", "cols"),
            P(),
            P(None, ("rows", "cols"), None),
            P(None, ("rows", "cols"), None),
            P(),
        ),
        out_specs=(P(("rows", "cols"), None), P(("rows", "cols"), None)),
        check_vma=False,
    )
```

profile of v0, /device:TPU:64, one launch (start us, length us, event | category | flops | bytes accessed | tf_op | source)
XLA Modules:
  0.0 281.9 jit_solution(1292776319024039563)
XLA Ops:
  0.6 3.3 %collective-permute-start.126 = (bf16[256,512]{1,0:T(8,128)(2,1)}, bf16[256,512]{1,0:T(8,128)(2,1)S(1)}, u32[]{:S(2)}, u32[]{:S(2)}) collective-permute-start(bf16[256,512]{1,0:T(8,128)(2,1)} %refs_0_.1), channel_id=1, source_target_pairs={{0,2},{1,3},{2,0},{3,1},{4,6},{5,7},{6,4},{7,5},{8,10},{9,11},{10,... | collective-permute-start | bytes 786440 | tf_op jit(solution)/shard_map/ppermute | solution.py:18
  3.9 0.7 collective-permute-start.125
  4.6 5.4 %collective-permute-start.124 = (bf16[256,512]{1,0:T(8,128)(2,1)}, bf16[256,512]{1,0:T(8,128)(2,1)S(1)}, u32[]{:S(2)}, u32[]{:S(2)}) collective-permute-start(bf16[256,512]{1,0:T(8,128)(2,1)} %refs_0_.1), channel_id=1, source_target_pairs={{0,4},{1,5},{2,6},{3,7},{4,0},{5,1},{6,2},{7,3},{8,12},{9,13},{10,... | collective-permute-start | bytes 786440 | tf_op jit(solution)/shard_map/ppermute | solution.py:18
  10.0 0.4 collective-permute-start.127
  10.4 1.2 slice.202
  12.2 0.0 copy-start.7
  12.2 35.8 %conditional.4 = (bf16[384,512]{1,0:T(8,128)(2,1)}) conditional(s32[]{:T(128)} %bitcast.2, bf16[1024,512]{1,0:T(8,128)(2,1)} %param.139, bf16[1024,512]{1,0:T(8,128)(2,1)} %param.139, bf16[1024,512]{1,0:T(8,128)(2,1)} %param.139, bf16[1024,512]{1,0:T(8,128)(2,1)} %param.139, bf16[1024,512]{1,0:T(8,128)(2,1)} %param.139, ...), branch_computations={%region_0.0_spmd, %region_1.0_spmd, %region_2.0_spmd, %region_3.0_... | conditional | bytes 2359344 | solution.py:230
  12.3 1.0 slice.138
  13.3 1.5 collective-permute-start.3
  14.8 22.2 %collective-permute-done.3 = bf16[384,512]{1,0:T(8,128)(2,1)} collective-permute-done((bf16[384,512]{1,0:T(8,128)(2,1)S(1)}, bf16[384,512]{1,0:T(8,128)(2,1)}, u32[]{:S(2)}, u32[]{:S(2)}) %collective-permute-start.3) | collective-permute-done | bytes 393248 | tf_op jit(solution)/shard_map/cond/branch_4_fun/ppermute | solution.py:18
  48.0 0.0 collective-permute-done.126.refs_2_
  48.0 0.0 collective-permute-done.125.refs_1_
  48.0 0.8 collective-permute-start.130
  48.8 2.7 collective-permute-start.129
  51.5 0.7 collective-permute-start.128
  52.2 0.1 copy.13.count
  52.3 40.3 %conditional.5 = (bf16[640,512]{1,0:T(8,128)(2,1)}) conditional(s32[]{:T(128)} %bitcast.2, bf16[1024,512]{1,0:T(8,128)(2,1)} %param.139, bf16[1024,512]{1,0:T(8,128)(2,1)} %param.139, bf16[1024,512]{1,0:T(8,128)(2,1)} %param.139, bf16[1024,512]{1,0:T(8,128)(2,1)} %param.139, bf16[1024,512]{1,0:T(8,128)(2,1)} %param.139, ...), branch_computations={%region_32.0_spmd, %region_33.0_spmd, %region_34.0_spmd, %region_3... | conditional | bytes 3932208 | solution.py:230
  52.4 1.2 slice.170
  53.6 3.6 %collective-permute-start.34 = (bf16[640,512]{1,0:T(8,128)(2,1)S(1)}, bf16[640,512]{1,0:T(8,128)(2,1)}, u32[]{:S(2)}, u32[]{:S(2)}) collective-permute-start(bf16[640,512]{1,0:T(8,128)(2,1)S(1)} %slice.170), channel_id=1, source_target_pairs={{0,32},{8,40},{16,48},{24,56},{32,0},{40,8},{48,16},{56,24},{64,96... | collective-permute-start | bytes 1966088 | tf_op jit(solution)/shard_map/cond/branch_4_fun/ppermute | solution.py:18
  57.2 27.0 %collective-permute-done.34 = bf16[640,512]{1,0:T(8,128)(2,1)} collective-permute-done((bf16[640,512]{1,0:T(8,128)(2,1)S(1)}, bf16[640,512]{1,0:T(8,128)(2,1)}, u32[]{:S(2)}, u32[]{:S(2)}) %collective-permute-start.34) | collective-permute-done | bytes 655392 | tf_op jit(solution)/shard_map/cond/branch_4_fun/ppermute | solution.py:18
  92.7 0.0 copy-start.3
  92.7 1.6 copy-done.3
  94.3 6.1 %stratum_0.1 = (bf16[256,512]{1,0:T(8,128)(2,1)S(1)}, bf16[256,512]{1,0:T(8,128)(2,1)S(1)}, bf16[256,512]{1,0:T(8,128)(2,1)S(1)}, bf16[256,512]{1,0:T(8,128)(2,1...) custom-call(s32[1]{0:T(128)} %bitcast.me, ...), custom_call_target="tpu_custom_call" | custom-call | flops 3221225472 | bytes 9437184 | tf_op jit(solution)/shard_map/stratum_0/pallas_call | solution.py:126
  100.4 1.4 collective-permute-start.134
  101.8 0.8 collective-permute-start.135
  102.6 2.6 collective-permute-start.136
  105.2 3.6 %collective-permute-start.138 = (bf16[384,512]{1,0:T(8,128)(2,1)S(1)}, bf16[384,512]{1,0:T(8,128)(2,1)S(1)}, u32[]{:S(2)}, u32[]{:S(2)}) collective-permute-start(bf16[384,512]{1,0:T(8,128)(2,1)S(1)} %get-tuple-element.315), channel_id=1, source_target_pairs={{0,248},{8,240},{16,232},{24,224},{32,216},{40,208},{48,200},{56,1... | collective-permute-start | bytes 1179656 | tf_op jit(solution)/shard_map/ppermute | solution.py:18
  108.8 0.9 collective-permute-done.134
  109.7 3.8 %collective-permute-done.135 = bf16[256,512]{1,0:T(8,128)(2,1)S(1)} collective-permute-done((bf16[256,512]{1,0:T(8,128)(2,1)S(1)}, bf16[256,512]{1,0:T(8,128)(2,1)S(1)}, u32[]{:S(2)}, u32[]{:S(2)}) %collective-permute-start.135) | collective-permute-done | bytes 262176 | tf_op jit(solution)/shard_map/ppermute | solution.py:18
  113.6 2.7 collective-permute-done.136
  116.2 0.1 add_convert_fusion.1
  116.3 3.7 %collective-permute-start.137 = (bf16[256,512]{1,0:T(8,128)(2,1)S(1)}, bf16[256,512]{1,0:T(8,128)(2,1)S(1)}, u32[]{:S(2)}, u32[]{:S(2)}) collective-permute-start(bf16[256,512]{1,0:T(8,128)(2,1)S(1)} %add_convert_fusion.1), channel_id=1, source_target_pairs={{0,4},{1,5},{2,6},{3,7},{4,0},{5,1},{6,2},{7,3},{8,12},{9,13},{10,... | collective-permute-start | bytes 786440 | tf_op jit(solution)/shard_map/ppermute | solution.py:18
  120.1 4.4 %collective-permute-start.132 = (bf16[256,512]{1,0:T(8,128)(2,1)S(1)}, bf16[256,512]{1,0:T(8,128)(2,1)S(1)}, u32[]{:S(2)}, u32[]{:S(2)}) collective-permute-start(bf16[256,512]{1,0:T(8,128)(2,1)S(1)} %get-tuple-element.309), channel_id=1, source_target_pairs={{0,2},{1,3},{2,0},{3,1},{4,6},{5,7},{6,4},{7,5},{8,10},{9,11},{10,... | collective-permute-start | bytes 786440 | tf_op jit(solution)/shard_map/ppermute | solution.py:18
  124.5 0.3 collective-permute-start.133
  124.9 13.1 %collective-permute-done.138.refs_8_ = bf16[384,512]{1,0:T(8,128)(2,1)S(1)} collective-permute-done((bf16[384,512]{1,0:T(8,128)(2,1)S(1)}, bf16[384,512]{1,0:T(8,128)(2,1)S(1)}, u32[]{:S(2)}, u32[]{:S(2)}) %collective-permute-start.138) | collective-permute-done | bytes 393248 | tf_op jit(solution)/shard_map/ppermute | solution.py:18
  138.0 0.3 fusion.2.refs_0_.refs_5_
  138.3 0.4 collective-permute-start.142
  138.7 1.0 collective-permute-start.141
  139.7 2.8 collective-permute-start.140
  142.5 2.9 %collective-permute-start.139 = (bf16[256,512]{1,0:T(8,128)(2,1)S(1)}, bf16[256,512]{1,0:T(8,128)(2,1)S(1)}, u32[]{:S(2)}, u32[]{:S(2)}) collective-permute-start(bf16[256,512]{1,0:T(8,128)(2,1)S(1)} %fusion.2.refs_0_.refs_5_), channel_id=1, source_target_pairs={{0,4},{1,5},{2,6},{3,7},{4,0},{5,1},{6,2},{7,3},{8,12},{9,13},{10,... | collective-permute-start | bytes 786440 | tf_op jit(solution)/shard_map/ppermute | solution.py:18
  145.4 8.3 %collective-permute-done.142.refs_3_ = bf16[256,512]{1,0:T(8,128)(2,1)S(1)} collective-permute-done((bf16[256,512]{1,0:T(8,128)(2,1)S(1)}, bf16[256,512]{1,0:T(8,128)(2,1)S(1)}, u32[]{:S(2)}, u32[]{:S(2)}) %collective-permute-start.142) | collective-permute-done | bytes 262176 | tf_op jit(solution)/shard_map/ppermute | solution.py:18
  153.7 0.6 collective-permute-done.140.refs_1_
  154.3 3.5 %collective-permute-done.139.refs_4_ = bf16[256,512]{1,0:T(8,128)(2,1)S(1)} collective-permute-done((bf16[256,512]{1,0:T(8,128)(2,1)S(1)}, bf16[256,512]{1,0:T(8,128)(2,1)S(1)}, u32[]{:S(2)}, u32[]{:S(2)}) %collective-permute-start.139) | collective-permute-done | bytes 262176 | tf_op jit(solution)/shard_map/ppermute | solution.py:18
  157.8 1.9 collective-permute-start.146
  159.7 0.7 collective-permute-start.145
  160.4 2.1 collective-permute-start.144
  162.5 1.7 collective-permute-start.143
  164.2 10.6 %collective-permute-done.145.refs_7_ = bf16[256,512]{1,0:T(8,128)(2,1)S(1)} collective-permute-done((bf16[256,512]{1,0:T(8,128)(2,1)S(1)}, bf16[256,512]{1,0:T(8,128)(2,1)S(1)}, u32[]{:S(2)}, u32[]{:S(2)}) %collective-permute-start.145) | collective-permute-done | bytes 262176 | tf_op jit(solution)/shard_map/ppermute | solution.py:18
  174.8 1.2 collective-permute-done.143.refs_5_
  176.0 12.3 %collective-permute-done.146.refs_9_ = bf16[640,512]{1,0:T(8,128)(2,1)S(1)} collective-permute-done((bf16[640,512]{1,0:T(8,128)(2,1)S(1)}, bf16[640,512]{1,0:T(8,128)(2,1)S(1)}, u32[]{:S(2)}, u32[]{:S(2)}) %collective-permute-start.146) | collective-permute-done | bytes 655392 | tf_op jit(solution)/shard_map/ppermute | solution.py:18
  188.3 5.8 %stratum_1.1 = (bf16[256,512]{1,0:T(8,128)(2,1)S(1)}, bf16[256,512]{1,0:T(8,128)(2,1)S(1)}, bf16[256,512]{1,0:T(8,128)(2,1)S(1)}, bf16[256,512]{1,0:T(8,128)(2,1...) custom-call(s32[1]{0:T(128)} %bitcast.me, ...), custom_call_target="tpu_custom_call" | custom-call | flops 3221225472 | bytes 9437184 | tf_op jit(solution)/shard_map/stratum_1/pallas_call | solution.py:126
  194.1 3.2 %collective-permute-start.147 = (bf16[256,512]{1,0:T(8,128)(2,1)}, bf16[256,512]{1,0:T(8,128)(2,1)}, u32[]{:S(2)}, u32[]{:S(2)}) collective-permute-start(bf16[256,512]{1,0:T(8,128)(2,1)} %get-tuple-element.327), channel_id=1, source_target_pairs={{0,1},{1,0},{2,3},{3,2},{4,5},{5,4},{6,7},{7,6},{8,9},{9,8},{10,11... | collective-permute-start | bytes 786440 | tf_op jit(solution)/shard_map/ppermute | solution.py:18
  197.3 0.6 collective-permute-start.148
  197.9 2.2 collective-permute-start.149
  200.1 12.7 %conditional.6 = (bf16[384,512]{1,0:T(8,128)(2,1)}) conditional(s32[]{:T(128)} %bitcast.2, bf16[384,512]{1,0:T(8,128)(2,1)S(1)} %get-tuple-element.330, bf16[384,512]{1,0:T(8,128)(2,1)S(1)} %get-tuple-element.330, bf16[384,512]{1,0:T(8,128)(2,1)S(1)} %get-tuple-element.330, ...), branch_computations={%region_64.0_spmd, %region_65.0_spmd, %region_66.0_spmd, %region_6... | conditional | bytes 1572912 | solution.py:230
  200.1 12.6 %collective-permute-done.66 = bf16[384,512]{1,0:T(8,128)(2,1)} collective-permute-done((bf16[384,512]{1,0:T(8,128)(2,1)S(1)}, bf16[384,512]{1,0:T(8,128)(2,1)}, u32[]{:S(2)}, u32[]{:S(2)}) %collective-permute-start.66) | collective-permute-done | bytes 393248 | tf_op jit(solution)/shard_map/cond/branch_4_fun/ppermute | solution.py:18
  212.8 1.0 collective-permute-done.149
  213.8 1.9 add_convert_fusion
  215.8 2.1 collective-permute-start.151
  217.8 2.6 collective-permute-start.152
  220.5 2.7 collective-permute-start.153
  223.2 24.0 %conditional.7 = (bf16[640,512]{1,0:T(8,128)(2,1)}) conditional(s32[]{:T(128)} %bitcast.2, bf16[640,512]{1,0:T(8,128)(2,1)S(1)} %get-tuple-element.339, bf16[640,512]{1,0:T(8,128)(2,1)S(1)} %get-tuple-element.339, bf16[640,512]{1,0:T(8,128)(2,1)S(1)} %get-tuple-element.339, ...), branch_computations={%region_96.0_spmd, %region_97.0_spmd, %region_98.0_spmd, %region_9... | conditional | bytes 2621488 | solution.py:230
  223.2 23.8 %collective-permute-done.97 = bf16[640,512]{1,0:T(8,128)(2,1)} collective-permute-done((bf16[640,512]{1,0:T(8,128)(2,1)S(1)}, bf16[640,512]{1,0:T(8,128)(2,1)}, u32[]{:S(2)}, u32[]{:S(2)}) %collective-permute-start.97) | collective-permute-done | bytes 655392 | tf_op jit(solution)/shard_map/cond/branch_4_fun/ppermute | solution.py:18
  247.3 34.2 %finish.1 = (bf16[256,512]{1,0:T(8,128)(2,1)}, bf16[1024,512]{1,0:T(8,128)(2,1)}) custom-call(f32[2]{0:T(128)S(1)} %copy-done.2, bf16[256,512]{1,0:T(8,128)(2,1)S(1)} %get-tuple-element.324.refs_0_, bf16[256,512]{1,0:T(8,128)(2,1)S(1)} %collective-permute-done.150.refs_1_, bf16[256,512]{1,0:T(8,128)(2,1)S(1)} %collective-permute-done.151.refs_2_, ...), custom_call_target="tpu_custom_call" | custom-call | tf_op jit(solution)/shard_map/finish/pallas_call | solution.py:186
  (34 shorter events, 0.1 us)
Async XLA Ops:
  0.6 47.4 %collective-permute-start.126 = (bf16[256,512]{1,0:T(8,128)(2,1)}, bf16[256,512]{1,0:T(8,128)(2,1)S(1)}, u32[]{:S(2)}, u32[]{:S(2)}) collective-permute-start(bf16[256,512]{1,0:T(8,128)(2,1)} %refs_0_.1), channel_id=1, source_target_pairs={{0,2},{1,3},{2,0},{3,1},{4,6},{5,7},{6,4},{7,5},{8,10},{9,11},{10,... | collective-permute-start | bytes 786440 | tf_op jit(solution)/shard_map/ppermute | solution.py:18
  3.9 44.1 %collective-permute-start.125 = (bf16[256,512]{1,0:T(8,128)(2,1)}, bf16[256,512]{1,0:T(8,128)(2,1)S(1)}, u32[]{:S(2)}, u32[]{:S(2)}) collective-permute-start(bf16[256,512]{1,0:T(8,128)(2,1)} %refs_0_.1), channel_id=1, source_target_pairs={{0,1},{1,0},{2,3},{3,2},{4,5},{5,4},{6,7},{7,6},{8,9},{9,8},{10,11... | collective-permute-start | bytes 786440 | tf_op jit(solution)/shard_map/ppermute | solution.py:18
  4.6 43.4 %collective-permute-start.124 = (bf16[256,512]{1,0:T(8,128)(2,1)}, bf16[256,512]{1,0:T(8,128)(2,1)S(1)}, u32[]{:S(2)}, u32[]{:S(2)}) collective-permute-start(bf16[256,512]{1,0:T(8,128)(2,1)} %refs_0_.1), channel_id=1, source_target_pairs={{0,4},{1,5},{2,6},{3,7},{4,0},{5,1},{6,2},{7,3},{8,12},{9,13},{10,... | collective-permute-start | bytes 786440 | tf_op jit(solution)/shard_map/ppermute | solution.py:18
  10.0 38.1 %collective-permute-start.127 = (bf16[256,512]{1,0:T(8,128)(2,1)}, bf16[256,512]{1,0:T(8,128)(2,1)S(1)}, u32[]{:S(2)}, u32[]{:S(2)}) collective-permute-start(bf16[256,512]{1,0:T(8,128)(2,1)} %refs_0_.1), channel_id=1, source_target_pairs={{0,3},{1,2},{2,1},{3,0},{4,7},{5,6},{6,5},{7,4},{8,11},{9,10},{10,... | collective-permute-start | bytes 786440 | tf_op jit(solution)/shard_map/ppermute | solution.py:18
  12.2 40.0 %copy-start.7 = (s32[2,1,1]{0,2,1:T(1,128)S(1)}, s32[2,1,1]{0,2,1:T(1,128)}, u32[]{:S(2)}) copy-start(s32[2,1,1]{0,2,1:T(1,128)} %param.143) | copy-start | bytes 28
  13.3 23.7 %collective-permute-start.3 = (bf16[384,512]{1,0:T(8,128)(2,1)S(1)}, bf16[384,512]{1,0:T(8,128)(2,1)}, u32[]{:S(2)}, u32[]{:S(2)}) collective-permute-start(bf16[384,512]{1,0:T(8,128)(2,1)S(1)} %slice.138), channel_id=1, source_target_pairs={{0,32},{8,40},{16,48},{24,56},{32,0},{40,8},{48,16},{56,24},{64,96... | collective-permute-start | bytes 1179656 | tf_op jit(solution)/shard_map/cond/branch_4_fun/ppermute | solution.py:18
  48.0 44.6 %collective-permute-start.130 = (bf16[256,512]{1,0:T(8,128)(2,1)S(1)}, bf16[256,512]{1,0:T(8,128)(2,1)S(1)}, u32[]{:S(2)}, u32[]{:S(2)}) collective-permute-start(bf16[256,512]{1,0:T(8,128)(2,1)S(1)} %collective-permute-done.124.refs_4_), channel_id=1, source_target_pairs={{0,3},{1,2},{2,1},{3,0},{4,7},{5,6},{6,5},{7,4},{8,11},{9,10},{10,... | collective-permute-start | bytes 786440 | tf_op jit(solution)/shard_map/ppermute | solution.py:18
  48.8 43.8 %collective-permute-start.129 = (bf16[256,512]{1,0:T(8,128)(2,1)S(1)}, bf16[256,512]{1,0:T(8,128)(2,1)S(1)}, u32[]{:S(2)}, u32[]{:S(2)}) collective-permute-start(bf16[256,512]{1,0:T(8,128)(2,1)S(1)} %collective-permute-done.124.refs_4_), channel_id=1, source_target_pairs={{0,2},{1,3},{2,0},{3,1},{4,6},{5,7},{6,4},{7,5},{8,10},{9,11},{10,... | collective-permute-start | bytes 786440 | tf_op jit(solution)/shard_map/ppermute | solution.py:18
  51.5 41.1 %collective-permute-start.128 = (bf16[256,512]{1,0:T(8,128)(2,1)S(1)}, bf16[256,512]{1,0:T(8,128)(2,1)S(1)}, u32[]{:S(2)}, u32[]{:S(2)}) collective-permute-start(bf16[256,512]{1,0:T(8,128)(2,1)S(1)} %collective-permute-done.124.refs_4_), channel_id=1, source_target_pairs={{0,1},{1,0},{2,3},{3,2},{4,5},{5,4},{6,7},{7,6},{8,9},{9,8},{10,11... | collective-permute-start | bytes 786440 | tf_op jit(solution)/shard_map/ppermute | solution.py:18
  52.3 40.3 %copy-start.1 = (bf16[256,512]{1,0:T(8,128)(2,1)S(1)}, bf16[256,512]{1,0:T(8,128)(2,1)}, u32[]{:S(2)}) copy-start(bf16[256,512]{1,0:T(8,128)(2,1)} %refs_0_.1) | copy-start | bytes 786436
  52.3 40.3 %copy-start.2 = (f32[2]{0:T(128)S(1)}, f32[2]{0:T(128)}, u32[]{:S(2)}) copy-start(f32[2]{0:T(128)} %step.5) | copy-start | bytes 28
  52.3 40.4 %copy-start.5 = (s32[2,1,1,16]{3,2,1,0:T(1,128)S(1)}, s32[2,1,1,16]{3,2,1,0:T(1,128)}, u32[]{:S(2)}) copy-start(s32[2,1,1,16]{3,2,1,0:T(1,128)} %row_pick.3) | copy-start | bytes 388
  52.3 40.4 %copy-start.6 = (s32[2,1,1,16]{3,2,1,0:T(1,128)S(1)}, s32[2,1,1,16]{3,2,1,0:T(1,128)}, u32[]{:S(2)}) copy-start(s32[2,1,1,16]{3,2,1,0:T(1,128)} %col_pick.3) | copy-start | bytes 388
  53.6 30.6 %collective-permute-start.34 = (bf16[640,512]{1,0:T(8,128)(2,1)S(1)}, bf16[640,512]{1,0:T(8,128)(2,1)}, u32[]{:S(2)}, u32[]{:S(2)}) collective-permute-start(bf16[640,512]{1,0:T(8,128)(2,1)S(1)} %slice.170), channel_id=1, source_target_pairs={{0,32},{8,40},{16,48},{24,56},{32,0},{40,8},{48,16},{56,24},{64,96... | collective-permute-start | bytes 1966088 | tf_op jit(solution)/shard_map/cond/branch_4_fun/ppermute | solution.py:18
  92.7 1.6 copy-start.3
  94.3 43.7 %copy-start = (bf16[2,256,512]{2,1,0:T(8,128)(2,1)S(1)}, bf16[2,256,512]{2,1,0:T(8,128)(2,1)}, u32[]{:S(2)}) copy-start(bf16[2,256,512]{2,1,0:T(8,128)(2,1)} %refs_6_.1) | copy-start | bytes 1572868
  94.3 94.0 %copy-start.4 = (bf16[2,1024,512]{2,1,0:T(8,128)(2,1)S(1)}, bf16[2,1024,512]{2,1,0:T(8,128)(2,1)}, u32[]{:S(2)}) copy-start(bf16[2,1024,512]{2,1,0:T(8,128)(2,1)} %refs_11_.3) | copy-start | bytes 6291460
  100.4 9.3 %collective-permute-start.134 = (bf16[256,512]{1,0:T(8,128)(2,1)S(1)}, bf16[256,512]{1,0:T(8,128)(2,1)S(1)}, u32[]{:S(2)}, u32[]{:S(2)}) collective-permute-start(bf16[256,512]{1,0:T(8,128)(2,1)S(1)} %get-tuple-element.312), channel_id=1, source_target_pairs={{0,1},{1,0},{2,3},{3,2},{4,5},{5,4},{6,7},{7,6},{8,9},{9,8},{10,11... | collective-permute-start | bytes 786440 | tf_op jit(solution)/shard_map/ppermute | solution.py:18
  101.8 11.7 %collective-permute-start.135 = (bf16[256,512]{1,0:T(8,128)(2,1)S(1)}, bf16[256,512]{1,0:T(8,128)(2,1)S(1)}, u32[]{:S(2)}, u32[]{:S(2)}) collective-permute-start(bf16[256,512]{1,0:T(8,128)(2,1)S(1)} %get-tuple-element.313), channel_id=1, source_target_pairs={{0,2},{1,3},{2,0},{3,1},{4,6},{5,7},{6,4},{7,5},{8,10},{9,11},{10,... | collective-permute-start | bytes 786440 | tf_op jit(solution)/shard_map/ppermute | solution.py:18
  102.6 13.6 %collective-permute-start.136 = (bf16[256,512]{1,0:T(8,128)(2,1)S(1)}, bf16[256,512]{1,0:T(8,128)(2,1)S(1)}, u32[]{:S(2)}, u32[]{:S(2)}) collective-permute-start(bf16[256,512]{1,0:T(8,128)(2,1)S(1)} %get-tuple-element.314), channel_id=1, source_target_pairs={{0,3},{1,2},{2,1},{3,0},{4,7},{5,6},{6,5},{7,4},{8,11},{9,10},{10,... | collective-permute-start | bytes 786440 | tf_op jit(solution)/shard_map/ppermute | solution.py:18
  105.2 32.7 %collective-permute-start.138 = (bf16[384,512]{1,0:T(8,128)(2,1)S(1)}, bf16[384,512]{1,0:T(8,128)(2,1)S(1)}, u32[]{:S(2)}, u32[]{:S(2)}) collective-permute-start(bf16[384,512]{1,0:T(8,128)(2,1)S(1)} %get-tuple-element.315), channel_id=1, source_target_pairs={{0,248},{8,240},{16,232},{24,224},{32,216},{40,208},{48,200},{56,1... | collective-permute-start | bytes 1179656 | tf_op jit(solution)/shard_map/ppermute | solution.py:18
  116.3 21.6 %collective-permute-start.137 = (bf16[256,512]{1,0:T(8,128)(2,1)S(1)}, bf16[256,512]{1,0:T(8,128)(2,1)S(1)}, u32[]{:S(2)}, u32[]{:S(2)}) collective-permute-start(bf16[256,512]{1,0:T(8,128)(2,1)S(1)} %add_convert_fusion.1), channel_id=1, source_target_pairs={{0,4},{1,5},{2,6},{3,7},{4,0},{5,1},{6,2},{7,3},{8,12},{9,13},{10,... | collective-permute-start | bytes 786440 | tf_op jit(solution)/shard_map/ppermute | solution.py:18
  120.1 17.9 %collective-permute-start.131 = (bf16[256,512]{1,0:T(8,128)(2,1)S(1)}, bf16[256,512]{1,0:T(8,128)(2,1)S(1)}, u32[]{:S(2)}, u32[]{:S(2)}) collective-permute-start(bf16[256,512]{1,0:T(8,128)(2,1)S(1)} %get-tuple-element.308), channel_id=1, source_target_pairs={{0,1},{1,0},{2,3},{3,2},{4,5},{5,4},{6,7},{7,6},{8,9},{9,8},{10,11... | collective-permute-start | bytes 786440 | tf_op jit(solution)/shard_map/ppermute | solution.py:18
  120.1 17.9 %collective-permute-start.132 = (bf16[256,512]{1,0:T(8,128)(2,1)S(1)}, bf16[256,512]{1,0:T(8,128)(2,1)S(1)}, u32[]{:S(2)}, u32[]{:S(2)}) collective-permute-start(bf16[256,512]{1,0:T(8,128)(2,1)S(1)} %get-tuple-element.309), channel_id=1, source_target_pairs={{0,2},{1,3},{2,0},{3,1},{4,6},{5,7},{6,4},{7,5},{8,10},{9,11},{10,... | collective-permute-start | bytes 786440 | tf_op jit(solution)/shard_map/ppermute | solution.py:18
  124.5 13.5 %collective-permute-start.133 = (bf16[256,512]{1,0:T(8,128)(2,1)S(1)}, bf16[256,512]{1,0:T(8,128)(2,1)S(1)}, u32[]{:S(2)}, u32[]{:S(2)}) collective-permute-start(bf16[256,512]{1,0:T(8,128)(2,1)S(1)} %get-tuple-element.310), channel_id=1, source_target_pairs={{0,3},{1,2},{2,1},{3,0},{4,7},{5,6},{6,5},{7,4},{8,11},{9,10},{10,... | collective-permute-start | bytes 786440 | tf_op jit(solution)/shard_map/ppermute | solution.py:18
  138.3 15.4 %collective-permute-start.142 = (bf16[256,512]{1,0:T(8,128)(2,1)S(1)}, bf16[256,512]{1,0:T(8,128)(2,1)S(1)}, u32[]{:S(2)}, u32[]{:S(2)}) collective-permute-start(bf16[256,512]{1,0:T(8,128)(2,1)S(1)} %fusion.2.refs_0_.refs_5_), channel_id=1, source_target_pairs={{0,3},{1,2},{2,1},{3,0},{4,7},{5,6},{6,5},{7,4},{8,11},{9,10},{10,... | collective-permute-start | bytes 786440 | tf_op jit(solution)/shard_map/ppermute | solution.py:18
  138.7 15.0 %collective-permute-start.141 = (bf16[256,512]{1,0:T(8,128)(2,1)S(1)}, bf16[256,512]{1,0:T(8,128)(2,1)S(1)}, u32[]{:S(2)}, u32[]{:S(2)}) collective-permute-start(bf16[256,512]{1,0:T(8,128)(2,1)S(1)} %fusion.2.refs_0_.refs_5_), channel_id=1, source_target_pairs={{0,2},{1,3},{2,0},{3,1},{4,6},{5,7},{6,4},{7,5},{8,10},{9,11},{10,... | collective-permute-start | bytes 786440 | tf_op jit(solution)/shard_map/ppermute | solution.py:18
  139.7 14.6 %collective-permute-start.140 = (bf16[256,512]{1,0:T(8,128)(2,1)S(1)}, bf16[256,512]{1,0:T(8,128)(2,1)S(1)}, u32[]{:S(2)}, u32[]{:S(2)}) collective-permute-start(bf16[256,512]{1,0:T(8,128)(2,1)S(1)} %fusion.2.refs_0_.refs_5_), channel_id=1, source_target_pairs={{0,1},{1,0},{2,3},{3,2},{4,5},{5,4},{6,7},{7,6},{8,9},{9,8},{10,11... | collective-permute-start | bytes 786440 | tf_op jit(solution)/shard_map/ppermute | solution.py:18
  142.5 15.3 %collective-permute-start.139 = (bf16[256,512]{1,0:T(8,128)(2,1)S(1)}, bf16[256,512]{1,0:T(8,128)(2,1)S(1)}, u32[]{:S(2)}, u32[]{:S(2)}) collective-permute-start(bf16[256,512]{1,0:T(8,128)(2,1)S(1)} %fusion.2.refs_0_.refs_5_), channel_id=1, source_target_pairs={{0,4},{1,5},{2,6},{3,7},{4,0},{5,1},{6,2},{7,3},{8,12},{9,13},{10,... | collective-permute-start | bytes 786440 | tf_op jit(solution)/shard_map/ppermute | solution.py:18
  157.8 30.5 %collective-permute-start.146 = (bf16[640,512]{1,0:T(8,128)(2,1)S(1)}, bf16[640,512]{1,0:T(8,128)(2,1)S(1)}, u32[]{:S(2)}, u32[]{:S(2)}) collective-permute-start(bf16[640,512]{1,0:T(8,128)(2,1)S(1)} %get-tuple-element.323), channel_id=1, source_target_pairs={{0,248},{8,240},{16,232},{24,224},{32,216},{40,208},{48,200},{56,1... | collective-permute-start | bytes 1966088 | tf_op jit(solution)/shard_map/ppermute | solution.py:18
  159.7 15.1 %collective-permute-start.145 = (bf16[256,512]{1,0:T(8,128)(2,1)S(1)}, bf16[256,512]{1,0:T(8,128)(2,1)S(1)}, u32[]{:S(2)}, u32[]{:S(2)}) collective-permute-start(bf16[256,512]{1,0:T(8,128)(2,1)S(1)} %collective-permute-done.139.refs_4_), channel_id=1, source_target_pairs={{0,3},{1,2},{2,1},{3,0},{4,7},{5,6},{6,5},{7,4},{8,11},{9,10},{10,... | collective-permute-start | bytes 786440 | tf_op jit(solution)/shard_map/ppermute | solution.py:18
  160.4 14.5 %collective-permute-start.144 = (bf16[256,512]{1,0:T(8,128)(2,1)S(1)}, bf16[256,512]{1,0:T(8,128)(2,1)S(1)}, u32[]{:S(2)}, u32[]{:S(2)}) collective-permute-start(bf16[256,512]{1,0:T(8,128)(2,1)S(1)} %collective-permute-done.139.refs_4_), channel_id=1, source_target_pairs={{0,2},{1,3},{2,0},{3,1},{4,6},{5,7},{6,4},{7,5},{8,10},{9,11},{10,... | collective-permute-start | bytes 786440 | tf_op jit(solution)/shard_map/ppermute | solution.py:18
  162.5 13.6 %collective-permute-start.143 = (bf16[256,512]{1,0:T(8,128)(2,1)S(1)}, bf16[256,512]{1,0:T(8,128)(2,1)S(1)}, u32[]{:S(2)}, u32[]{:S(2)}) collective-permute-start(bf16[256,512]{1,0:T(8,128)(2,1)S(1)} %collective-permute-done.139.refs_4_), channel_id=1, source_target_pairs={{0,1},{1,0},{2,3},{3,2},{4,5},{5,4},{6,7},{7,6},{8,9},{9,8},{10,11... | collective-permute-start | bytes 786440 | tf_op jit(solution)/shard_map/ppermute | solution.py:18
  194.1 18.7 %collective-permute-start.147 = (bf16[256,512]{1,0:T(8,128)(2,1)}, bf16[256,512]{1,0:T(8,128)(2,1)}, u32[]{:S(2)}, u32[]{:S(2)}) collective-permute-start(bf16[256,512]{1,0:T(8,128)(2,1)} %get-tuple-element.327), channel_id=1, source_target_pairs={{0,1},{1,0},{2,3},{3,2},{4,5},{5,4},{6,7},{7,6},{8,9},{9,8},{10,11... | collective-permute-start | bytes 786440 | tf_op jit(solution)/shard_map/ppermute | solution.py:18
  197.3 15.5 %collective-permute-start.148 = (bf16[256,512]{1,0:T(8,128)(2,1)S(1)}, bf16[256,512]{1,0:T(8,128)(2,1)}, u32[]{:S(2)}, u32[]{:S(2)}) collective-permute-start(bf16[256,512]{1,0:T(8,128)(2,1)S(1)} %get-tuple-element.328), channel_id=1, source_target_pairs={{0,2},{1,3},{2,0},{3,1},{4,6},{5,7},{6,4},{7,5},{8,10},{9,11},{10,... | collective-permute-start | bytes 786440 | tf_op jit(solution)/shard_map/ppermute | solution.py:18
  197.9 15.9 %collective-permute-start.149 = (bf16[256,512]{1,0:T(8,128)(2,1)S(1)}, bf16[256,512]{1,0:T(8,128)(2,1)}, u32[]{:S(2)}, u32[]{:S(2)}) collective-permute-start(bf16[256,512]{1,0:T(8,128)(2,1)S(1)} %get-tuple-element.329), channel_id=1, source_target_pairs={{0,3},{1,2},{2,1},{3,0},{4,7},{5,6},{6,5},{7,4},{8,11},{9,10},{10,... | collective-permute-start | bytes 786440 | tf_op jit(solution)/shard_map/ppermute | solution.py:18
  200.1 12.6 %collective-permute-start.66 = (bf16[384,512]{1,0:T(8,128)(2,1)S(1)}, bf16[384,512]{1,0:T(8,128)(2,1)}, u32[]{:S(2)}, u32[]{:S(2)}) collective-permute-start(bf16[384,512]{1,0:T(8,128)(2,1)S(1)} %param.68), channel_id=1, source_target_pairs={{0,216},{8,208},{16,200},{24,192},{32,248},{40,240},{48,232},{56,2... | collective-permute-start | bytes 1179656 | tf_op jit(solution)/shard_map/cond/branch_4_fun/ppermute | solution.py:18
  215.8 31.5 %collective-permute-start.150 = (bf16[256,512]{1,0:T(8,128)(2,1)S(1)}, bf16[256,512]{1,0:T(8,128)(2,1)S(1)}, u32[]{:S(2)}, u32[]{:S(2)}) collective-permute-start(bf16[256,512]{1,0:T(8,128)(2,1)S(1)} %get-tuple-element.332), channel_id=1, source_target_pairs={{0,1},{1,0},{2,3},{3,2},{4,5},{5,4},{6,7},{7,6},{8,9},{9,8},{10,11... | collective-permute-start | bytes 786440 | tf_op jit(solution)/shard_map/ppermute | solution.py:18
  215.8 31.5 %collective-permute-start.151 = (bf16[256,512]{1,0:T(8,128)(2,1)S(1)}, bf16[256,512]{1,0:T(8,128)(2,1)S(1)}, u32[]{:S(2)}, u32[]{:S(2)}) collective-permute-start(bf16[256,512]{1,0:T(8,128)(2,1)S(1)} %get-tuple-element.334), channel_id=1, source_target_pairs={{0,2},{1,3},{2,0},{3,1},{4,6},{5,7},{6,4},{7,5},{8,10},{9,11},{10,... | collective-permute-start | bytes 786440 | tf_op jit(solution)/shard_map/ppermute | solution.py:18
  217.8 29.4 %collective-permute-start.152 = (bf16[256,512]{1,0:T(8,128)(2,1)S(1)}, bf16[256,512]{1,0:T(8,128)(2,1)S(1)}, u32[]{:S(2)}, u32[]{:S(2)}) collective-permute-start(bf16[256,512]{1,0:T(8,128)(2,1)S(1)} %get-tuple-element.336), channel_id=1, source_target_pairs={{0,3},{1,2},{2,1},{3,0},{4,7},{5,6},{6,5},{7,4},{8,11},{9,10},{10,... | collective-permute-start | bytes 786440 | tf_op jit(solution)/shard_map/ppermute | solution.py:18
  220.5 26.8 %collective-permute-start.153 = (bf16[256,512]{1,0:T(8,128)(2,1)}, bf16[256,512]{1,0:T(8,128)(2,1)S(1)}, u32[]{:S(2)}, u32[]{:S(2)}) collective-permute-start(bf16[256,512]{1,0:T(8,128)(2,1)} %add_convert_fusion), channel_id=1, source_target_pairs={{0,4},{1,5},{2,6},{3,7},{4,0},{5,1},{6,2},{7,3},{8,12},{9,13},{10,... | collective-permute-start | bytes 786440 | tf_op jit(solution)/shard_map/ppermute | solution.py:18
  223.2 23.9 %collective-permute-start.97 = (bf16[640,512]{1,0:T(8,128)(2,1)S(1)}, bf16[640,512]{1,0:T(8,128)(2,1)}, u32[]{:S(2)}, u32[]{:S(2)}) collective-permute-start(bf16[640,512]{1,0:T(8,128)(2,1)S(1)} %param.100), channel_id=1, source_target_pairs={{0,216},{8,208},{16,200},{24,192},{32,248},{40,240},{48,232},{56,2... | collective-permute-start | bytes 1966088 | tf_op jit(solution)/shard_map/cond/branch_4_fun/ppermute | solution.py:18
where the time goes:
time: 286 us; the launch traced here: 282 us
  waiting for transfers between devices  144 us (50%)
  starting transfers between devices  62.8 us (22%)
  Pallas kernels  46.1 us (16%)
  loops' own time  19.9 us (7%)
  local copies, waits for them, and re-layouts  5.13 us (2%)
    ppermute x34, waiting for transfers between devices, swap(): lax.ppermute(value, axis, [(i, i ^ mask) for i in range(lax.axis_size(axi...  144 us
    ppermute x34, starting transfers between devices, swap(): lax.ppermute(value, axis, [(i, i ^ mask) for i in range(lax.axis_size(axi...  62.8 us
    pallas_call x1, Pallas kernels, finish(): pl.pallas_call(finish_kernel, out_shape=[jax.ShapeDtypeStruct(shard.shape...  34.2 us
    another operation x4, loops' own time, route(): lax.switch(first, [functools.partial(branch, k ^ flip) for k in range(blo...  19.9 us
    pallas_call x2, Pallas kernels, stratum_step(): pl.pallas_call(functools.partial(stratum_kernel, stratum), out_shape=[par...  11.9 us
  transfers between devices with their start and end apart: 34, of which 15 were waited for; matrix products, arithmetic and copies ran while one was open for 1% of the time, Pallas kernels for 0%

commit v1 on v0

--- a/solution.py
+++ b/solution.py
@@ -45,11 +45,10 @@
     q_out, (va_out, vb_out) = refs[PEERS + 4 : 2 * PEERS + 4], refs[2 * PEERS + 4 : 2 * PEERS + 6]
     u_s, v_s, t_s, n_s, r_acc, c_acc, q_s, u_sem, v_sem, t_sem, n_sem, o_sem = refs[2 * PEERS + 6 :]
     n_group = t_s.shape[0] // GROUP
-    cut = va_in.shape[0]
-    spans = (pl.ds(0, cut), pl.ds(cut, v_s.shape[0] - cut))
     loads = [pltpu.make_async_copy(u_in[k], u_s.at[k], u_sem.at[k]) for k in range(PEERS)]
     for i, v_in in enumerate((va_in, vb_in)):
-        loads.append(pltpu.make_async_copy(v_in, v_s.at[spans[i]], v_sem.at[i]))
+        span = pl.ds(i * va_in.shape[0], v_in.shape[0])
+        loads.append(pltpu.make_async_copy(v_in, v_s.at[span], v_sem.at[i]))
 
     def tile_load(i):
         span = pl.ds(i * GROUP, GROUP)
@@ -102,7 +101,8 @@
     root = jnp.sqrt(jnp.full((1, 1), h, jnp.float32))
     noise_load.wait()
     for i, v_out in enumerate((va_out, vb_out)):
-        for low in range(spans[i].start, spans[i].start + spans[i].size, TILE // 2):
+        first = i * va_out.shape[0]
+        for low in range(first, first + v_out.shape[0], TILE // 2):
             rows = pl.ds(low, TILE // 2)
             current = wide(v_s[rows])
             moved = (
@@ -111,13 +111,14 @@
                 + root * wide(n_s[rows])
             )
             v_s[rows] = moved.astype(jnp.bfloat16)
-        stores.append(pltpu.make_async_copy(v_s.at[spans[i]], v_out, o_sem.at[PEERS + i]))
+        span = pl.ds(first, v_out.shape[0])
+        stores.append(pltpu.make_async_copy(v_s.at[span], v_out, o_sem.at[PEERS + i]))
         stores[-1].start()
     for copy in stores:
         copy.wait()
 
 
-def stratum_step(stratum, me, step_sizes, tile_rows, tile_cols, tile_counts, rows, halves, tiles, noise):
+def stratum_step(stratum, me, step_sizes, tile_rows, tile_cols, tile_counts, rows, halves, cut, tiles, noise):
     n_col, rank = noise.shape[1:]
     n_slot = tiles.shape[3]
     smem = pl.BlockSpec(memory_space=pltpu.SMEM)
@@ -126,7 +127,7 @@
     out = pl.pallas_call(
         functools.partial(stratum_kernel, stratum),
         out_shape=[part] * PEERS
-        + [jax.ShapeDtypeStruct(v.shape, jnp.bfloat16) for v in halves],
+        + [jax.ShapeDtypeStruct((n, rank), jnp.bfloat16) for n in (cut, n_col - cut)],
         in_specs=[smem] * 5 + [free] * (PEERS + 4),
         out_specs=[free] * (PEERS + 2),
         scratch_shapes=[
@@ -143,7 +144,7 @@
             pltpu.SemaphoreType.DMA((1,)),
             pltpu.SemaphoreType.DMA((PEERS + 2,)),
         ],
-        compiler_params=pltpu.CompilerParams(vmem_limit_bytes=46 * 1024 * 1024),
+        compiler_params=pltpu.CompilerParams(vmem_limit_bytes=48 * 1024 * 1024),
         cost_estimate=pl.CostEstimate(
             flops=6 * n_slot * TILE * TILE * rank, bytes_accessed=9 << 20, transcendentals=0
         ),
@@ -154,20 +155,26 @@
 
 def finish_kernel(step, *refs):
     part_in, (shard, noise, va_in, vb_in) = refs[:5], refs[5:9]
-    row_out, col_out, part_s, own_s, sem, col_sem = refs[9:]
+    row_out, col_out, part_s, own_s, v_s, sem, col_sem = refs[9:]
     stratum = noise.shape[0] - 1
     cut = va_in.shape[0]
-    copies = [
-        pltpu.make_async_copy(va_in, col_out.at[pl.ds(0, cut)], col_sem.at[0]),
-        pltpu.make_async_copy(
-            vb_in, col_out.at[pl.ds(cut, vb_in.shape[0])], col_sem.at[1]
-        ),
+    spans = (pl.ds(0, cut), pl.ds(cut, vb_in.shape[0]))
+    pieces = [
+        pltpu.make_async_copy(v_in, v_s.at[span], col_sem.at[i])
+        for i, (v_in, span) in enumerate(zip((va_in, vb_in), spans))
+    ]
+    stores = [
+        pltpu.make_async_copy(v_s.at[span], col_out.at[span], col_sem.at[2 + i])
+        for i, span in enumerate(spans)
     ]
     loads = [pltpu.make_async_copy(part_in[i], part_s.at[i], sem.at[i]) for i in range(5)]
     loads.append(pltpu.make_async_copy(shard, own_s.at[0], sem.at[5]))
     loads.append(pltpu.make_async_copy(noise.at[stratum], own_s.at[1], sem.at[6]))
-    for copy in copies + loads:
+    for copy in pieces + loads:
         copy.start()
+    for piece, store in zip(pieces, stores):
+        piece.wait()
+        store.start()
     for copy in loads:
         copy.wait()
     total = wide(part_s[0]) + wide(part_s[1]) + wide(part_s[2]) + wide(part_s[3]) + wide(part_s[4])
@@ -176,8 +183,8 @@
     current = wide(own_s[0])
     moved = current + (0.5 * h) * (total - prior_precision * current) + root * wide(own_s[1])
     row_out[...] = moved.astype(jnp.bfloat16)
-    for copy in copies:
-        copy.wait()
+    for store in stores:
+        store.wait()
 
 
 def finish(step_sizes, terms, shard, row_noise, upper, lower):
@@ -194,8 +201,9 @@
         scratch_shapes=[
             pltpu.VMEM((5,) + shard.shape, jnp.bfloat16),
             pltpu.VMEM((2,) + shard.shape, jnp.bfloat16),
+            pltpu.VMEM(panel, jnp.bfloat16),
             pltpu.SemaphoreType.DMA((7,)),
-            pltpu.SemaphoreType.DMA((2,)),
+            pltpu.SemaphoreType.DMA((4,)),
         ],
         compiler_params=pltpu.CompilerParams(vmem_limit_bytes=16 * 1024 * 1024),
         name="finish",
@@ -231,9 +239,19 @@
             first, [functools.partial(branch, k ^ flip) for k in range(blocks)], *operands
         )
 
-    def kernel(stratum, rows, halves):
+    def kernel(stratum, rows, halves, cut_out):
         return stratum_step(
-            stratum, me, step_sizes, tile_rows, tile_cols, tile_counts, rows, halves, tiles, col_noise
+            stratum,
+            me,
+            step_sizes,
+            tile_rows,
+            tile_cols,
+            tile_counts,
+            rows,
+            halves,
+            cut_out,
+            tiles,
+            col_noise,
         )
 
     partner = swap(row_factor, "cols", 4)
@@ -242,13 +260,14 @@
     partner, upper, near = lax.optimization_barrier((partner, upper, near))
     far = swap_near(partner, 0)
     lower = route(lambda k, v: enter(k, slice(cut, None), v), 0, after(col_factor, partner))
-    parts, halves = kernel(0, [row_factor] + near + [partner] + far, (upper, lower))
+    parts, halves = kernel(0, [row_factor] + near + [partner] + far, (upper, lower), col_factor.shape[0] - cut)
 
     far = swap_near(parts, 4)
     upper = swap(halves[0], "rows", blocks - 1)
-    near = swap_near(parts, 0)
     far_sum = wide(parts[4]) + wide(far[0]) + wide(far[1]) + wide(far[2])
-    partner = swap(far_sum.astype(jnp.bfloat16), "cols", 4)
+    far_sum = far_sum.astype(jnp.bfloat16)
+    partner = swap(far_sum, "cols", 4)
+    near = swap_near([after(part, far_sum) for part in parts[:4]], 0)
     partner, upper = lax.optimization_barrier((partner, upper))
     total = wide(parts[0]) + wide(near[0]) + wide(near[1]) + wide(near[2]) + wide(partner)
     shard = langevin(row_factor, total, row_noise[0], step_sizes[0]).astype(jnp.bfloat16)
@@ -258,7 +277,7 @@
     partner, near = lax.optimization_barrier((partner, near))
     far = swap_near(partner, 0)
     lower = swap(after(halves[1], partner), "rows", blocks - 1)
-    parts, halves = kernel(1, [shard] + near + [partner] + far, (upper, lower))
+    parts, halves = kernel(1, [shard] + near + [partner] + far, (upper, lower), cut)
 
     far = swap_near(parts, 4)
     upper = route(leave, blocks - 1, halves[0])

time: 286 us -> 260 us (0.909)
  Pallas kernels: 46.1 us -> 14.3 us
  waiting for transfers between devices: 144 us -> 154 us
  starting transfers between devices: 62.8 us -> 59.6 us
    pallas_call x1, Pallas kernels: 34.2 us -> 3.39 us  [finish(): pl.pallas_call(finish_kernel, out_shape=[jax.ShapeDtypeStruct(shard.shape...]
    ppermute x34, waiting for transfers between devices: 144 us -> 154 us  [swap(): lax.ppermute(value, axis, [(i, i ^ mask) for i in range(lax.axis_size(axi...]
    ppermute x34, starting transfers between devices: 62.8 us -> 59.6 us  [swap(): lax.ppermute(value, axis, [(i, i ^ mask) for i in range(lax.axis_size(axi...]
  transfers between devices with their start and end apart: 34 -> 34, of which waited for: 15 -> 14; matrix products, arithmetic and copies ran while one was open for 1% -> 1% of each run, Pallas kernels for 0% -> 0%
where the time goes in v1:
time: 260 us; the launch traced here: 256 us
  waiting for transfers between devices  154 us (59%)
  starting transfers between devices  59.6 us (23%)
  loops' own time  19.9 us (8%)
  Pallas kernels  14.3 us (6%)
  local copies, waits for them, and re-layouts  3.52 us (1%)
    ppermute x34, waiting for transfers between devices, swap(): lax.ppermute(value, axis, [(i, i ^ mask) for i in range(lax.axis_size(axi...  154 us
    ppermute x34, starting transfers between devices, swap(): lax.ppermute(value, axis, [(i, i ^ mask) for i in range(lax.axis_size(axi...  59.6 us
    another operation x4, loops' own time, route(): lax.switch(first, [functools.partial(branch, k ^ flip) for k in range(blo...  19.9 us
    pallas_call x2, Pallas kernels, stratum_step(): pl.pallas_call(functools.partial(stratum_kernel, stratum), out_shape=[par...  10.9 us
  transfers between devices with their start and end apart: 34, of which 14 were waited for; matrix products, arithmetic and copies ran while one was open for 1% of the time, Pallas kernels for 0%

profile of v1, /device:TPU:64, one launch (start us, length us, event | category | flops | bytes accessed | tf_op | source)
XLA Modules:
  0.0 255.8 jit_solution(15264171905162520477)
XLA Ops:
  0.6 3.3 %collective-permute-start.126 = (bf16[256,512]{1,0:T(8,128)(2,1)}, bf16[256,512]{1,0:T(8,128)(2,1)S(1)}, u32[]{:S(2)}, u32[]{:S(2)}) collective-permute-start(bf16[256,512]{1,0:T(8,128)(2,1)} %refs_0_.1), channel_id=1, source_target_pairs={{0,2},{1,3},{2,0},{3,1},{4,6},{5,7},{6,4},{7,5},{8,10},{9,11},{10,... | collective-permute-start | bytes 786440 | tf_op jit(solution)/shard_map/ppermute | solution.py:18
  3.9 0.7 collective-permute-start.125
  4.6 5.4 %collective-permute-start.124 = (bf16[256,512]{1,0:T(8,128)(2,1)}, bf16[256,512]{1,0:T(8,128)(2,1)S(1)}, u32[]{:S(2)}, u32[]{:S(2)}) collective-permute-start(bf16[256,512]{1,0:T(8,128)(2,1)} %refs_0_.1), channel_id=1, source_target_pairs={{0,4},{1,5},{2,6},{3,7},{4,0},{5,1},{6,2},{7,3},{8,12},{9,13},{10,... | collective-permute-start | bytes 786440 | tf_op jit(solution)/shard_map/ppermute | solution.py:18
  10.0 0.4 collective-permute-start.127
  10.4 1.2 slice.202
  12.2 0.0 copy-start.5
  12.2 35.7 %conditional.4 = (bf16[384,512]{1,0:T(8,128)(2,1)}) conditional(s32[]{:T(128)} %bitcast.2, bf16[1024,512]{1,0:T(8,128)(2,1)} %param.139, bf16[1024,512]{1,0:T(8,128)(2,1)} %param.139, bf16[1024,512]{1,0:T(8,128)(2,1)} %param.139, bf16[1024,512]{1,0:T(8,128)(2,1)} %param.139, bf16[1024,512]{1,0:T(8,128)(2,1)} %param.139, ...), branch_computations={%region_0.0_spmd, %region_1.0_spmd, %region_2.0_spmd, %region_3.0_... | conditional | bytes 2359344 | solution.py:238
  12.3 1.0 slice.147
  13.3 1.1 collective-permute-start.12
  14.4 22.6 %collective-permute-done.12 = bf16[384,512]{1,0:T(8,128)(2,1)} collective-permute-done((bf16[384,512]{1,0:T(8,128)(2,1)S(1)}, bf16[384,512]{1,0:T(8,128)(2,1)}, u32[]{:S(2)}, u32[]{:S(2)}) %collective-permute-start.12) | collective-permute-done | bytes 393248 | tf_op jit(solution)/shard_map/cond/branch_13_fun/ppermute | solution.py:18
  47.9 0.0 collective-permute-done.126.refs_2_
  47.9 0.0 collective-permute-done.125.refs_1_
  48.0 0.0 collective-permute-done.127.refs_3_
  48.0 0.8 collective-permute-start.130
  48.8 2.7 %collective-permute-start.129 = (bf16[256,512]{1,0:T(8,128)(2,1)S(1)}, bf16[256,512]{1,0:T(8,128)(2,1)S(1)}, u32[]{:S(2)}, u32[]{:S(2)}) collective-permute-start(bf16[256,512]{1,0:T(8,128)(2,1)S(1)} %collective-permute-done.124.refs_4_), channel_id=1, source_target_pairs={{0,2},{1,3},{2,0},{3,1},{4,6},{5,7},{6,4},{7,5},{8,10},{9,11},{10,... | collective-permute-start | bytes 786440 | tf_op jit(solution)/shard_map/ppermute | solution.py:18
  51.4 0.7 collective-permute-start.128
  52.1 0.1 copy.13.count
  52.2 41.5 %conditional.5 = (bf16[640,512]{1,0:T(8,128)(2,1)}) conditional(s32[]{:T(128)} %bitcast.2, bf16[1024,512]{1,0:T(8,128)(2,1)} %param.139, bf16[1024,512]{1,0:T(8,128)(2,1)} %param.139, bf16[1024,512]{1,0:T(8,128)(2,1)} %param.139, bf16[1024,512]{1,0:T(8,128)(2,1)} %param.139, bf16[1024,512]{1,0:T(8,128)(2,1)} %param.139, ...), branch_computations={%region_32.0_spmd, %region_33.0_spmd, %region_34.0_spmd, %region_3... | conditional | bytes 3932208 | solution.py:238
  52.3 1.2 slice.179
  53.5 3.4 %collective-permute-start.43 = (bf16[640,512]{1,0:T(8,128)(2,1)S(1)}, bf16[640,512]{1,0:T(8,128)(2,1)}, u32[]{:S(2)}, u32[]{:S(2)}) collective-permute-start(bf16[640,512]{1,0:T(8,128)(2,1)S(1)} %slice.179), channel_id=1, source_target_pairs={{0,104},{8,96},{16,120},{24,112},{32,72},{40,64},{48,88},{56,80},{... | collective-permute-start | bytes 1966088 | tf_op jit(solution)/shard_map/cond/branch_13_fun/ppermute | solution.py:18
  56.9 28.5 %collective-permute-done.43 = bf16[640,512]{1,0:T(8,128)(2,1)} collective-permute-done((bf16[640,512]{1,0:T(8,128)(2,1)S(1)}, bf16[640,512]{1,0:T(8,128)(2,1)}, u32[]{:S(2)}, u32[]{:S(2)}) %collective-permute-start.43) | collective-permute-done | bytes 655392 | tf_op jit(solution)/shard_map/cond/branch_13_fun/ppermute | solution.py:18
  93.8 0.0 collective-permute-done.129.refs_6_
  93.8 0.0 collective-permute-done.128.refs_5_
  93.8 0.0 copy-start
  93.8 6.1 %stratum_0.1 = (bf16[256,512]{1,0:T(8,128)(2,1)S(1)}, bf16[256,512]{1,0:T(8,128)(2,1)S(1)}, bf16[256,512]{1,0:T(8,128)(2,1)S(1)}, bf16[256,512]{1,0:T(8,128)(2,1...) custom-call(s32[1]{0:T(128)} %bitcast.me, ...), custom_call_target="tpu_custom_call" | custom-call | flops 3221225472 | bytes 9437184 | tf_op jit(solution)/shard_map/stratum_0/pallas_call | solution.py:127
  99.9 3.5 %collective-permute-start.131 = (bf16[256,512]{1,0:T(8,128)(2,1)S(1)}, bf16[256,512]{1,0:T(8,128)(2,1)S(1)}, u32[]{:S(2)}, u32[]{:S(2)}) collective-permute-start(bf16[256,512]{1,0:T(8,128)(2,1)S(1)} %get-tuple-element.313), channel_id=1, source_target_pairs={{0,1},{1,0},{2,3},{3,2},{4,5},{5,4},{6,7},{7,6},{8,9},{9,8},{10,11... | collective-permute-start | bytes 786440 | tf_op jit(solution)/shard_map/ppermute | solution.py:18
  103.4 0.0 collective-permute-start.132
  103.4 2.8 %collective-permute-start.133 = (bf16[256,512]{1,0:T(8,128)(2,1)S(1)}, bf16[256,512]{1,0:T(8,128)(2,1)S(1)}, u32[]{:S(2)}, u32[]{:S(2)}) collective-permute-start(bf16[256,512]{1,0:T(8,128)(2,1)S(1)} %get-tuple-element.315), channel_id=1, source_target_pairs={{0,3},{1,2},{2,1},{3,0},{4,7},{5,6},{6,5},{7,4},{8,11},{9,10},{10,... | collective-permute-start | bytes 786440 | tf_op jit(solution)/shard_map/ppermute | solution.py:18
  106.2 4.1 %collective-permute-done.131 = bf16[256,512]{1,0:T(8,128)(2,1)S(1)} collective-permute-done((bf16[256,512]{1,0:T(8,128)(2,1)S(1)}, bf16[256,512]{1,0:T(8,128)(2,1)S(1)}, u32[]{:S(2)}, u32[]{:S(2)}) %collective-permute-start.131) | collective-permute-done | bytes 262176 | tf_op jit(solution)/shard_map/ppermute | solution.py:18
  110.3 4.0 %collective-permute-done.132 = bf16[256,512]{1,0:T(8,128)(2,1)S(1)} collective-permute-done((bf16[256,512]{1,0:T(8,128)(2,1)S(1)}, bf16[256,512]{1,0:T(8,128)(2,1)S(1)}, u32[]{:S(2)}, u32[]{:S(2)}) %collective-permute-start.132) | collective-permute-done | bytes 262176 | tf_op jit(solution)/shard_map/ppermute | solution.py:18
  114.3 2.6 %collective-permute-done.133 = bf16[256,512]{1,0:T(8,128)(2,1)S(1)} collective-permute-done((bf16[256,512]{1,0:T(8,128)(2,1)S(1)}, bf16[256,512]{1,0:T(8,128)(2,1)S(1)}, u32[]{:S(2)}, u32[]{:S(2)}) %collective-permute-start.133) | collective-permute-done | bytes 262176 | tf_op jit(solution)/shard_map/ppermute | solution.py:18
  116.9 0.1 add_convert_fusion.1
  117.0 3.3 %collective-permute-start.137 = (bf16[256,512]{1,0:T(8,128)(2,1)S(1)}, bf16[256,512]{1,0:T(8,128)(2,1)S(1)}, u32[]{:S(2)}, u32[]{:S(2)}) collective-permute-start(bf16[256,512]{1,0:T(8,128)(2,1)S(1)} %add_convert_fusion.1), channel_id=1, source_target_pairs={{0,4},{1,5},{2,6},{3,7},{4,0},{5,1},{6,2},{7,3},{8,12},{9,13},{10,... | collective-permute-start | bytes 786440 | tf_op jit(solution)/shard_map/ppermute | solution.py:18
  120.3 1.9 collective-permute-start.135
  122.2 2.8 %collective-permute-start.136 = (bf16[256,512]{1,0:T(8,128)(2,1)S(1)}, bf16[256,512]{1,0:T(8,128)(2,1)S(1)}, u32[]{:S(2)}, u32[]{:S(2)}) collective-permute-start(bf16[256,512]{1,0:T(8,128)(2,1)S(1)} %get-tuple-element.320), channel_id=1, source_target_pairs={{0,3},{1,2},{2,1},{3,0},{4,7},{5,6},{6,5},{7,4},{8,11},{9,10},{10,... | collective-permute-start | bytes 786440 | tf_op jit(solution)/shard_map/ppermute | solution.py:18
  125.1 13.8 %collective-permute-done.137 = bf16[256,512]{1,0:T(8,128)(2,1)S(1)} collective-permute-done((bf16[256,512]{1,0:T(8,128)(2,1)S(1)}, bf16[256,512]{1,0:T(8,128)(2,1)S(1)}, u32[]{:S(2)}, u32[]{:S(2)}) %collective-permute-start.137) | collective-permute-done | bytes 262176 | tf_op jit(solution)/shard_map/ppermute | solution.py:18
  138.9 15.9 %collective-permute-done.138.refs_8_ = bf16[640,512]{1,0:T(8,128)(2,1)S(1)} collective-permute-done((bf16[640,512]{1,0:T(8,128)(2,1)S(1)}, bf16[640,512]{1,0:T(8,128)(2,1)S(1)}, u32[]{:S(2)}, u32[]{:S(2)}) %collective-permute-start.138) | collective-permute-done | bytes 655392 | tf_op jit(solution)/shard_map/ppermute | solution.py:18
  154.8 0.3 fusion.2.refs_0_.refs_5_
  155.1 0.6 collective-permute-start.142
  155.7 2.3 collective-permute-start.141
  158.0 1.3 collective-permute-start.140
  159.3 8.5 %collective-permute-done.142.refs_3_ = bf16[256,512]{1,0:T(8,128)(2,1)S(1)} collective-permute-done((bf16[256,512]{1,0:T(8,128)(2,1)S(1)}, bf16[256,512]{1,0:T(8,128)(2,1)S(1)}, u32[]{:S(2)}, u32[]{:S(2)}) %collective-permute-start.142) | collective-permute-done | bytes 262176 | tf_op jit(solution)/shard_map/ppermute | solution.py:18
  167.8 0.6 collective-permute-done.140.refs_1_
  168.4 7.7 %collective-permute-done.139.refs_4_ = bf16[256,512]{1,0:T(8,128)(2,1)S(1)} collective-permute-done((bf16[256,512]{1,0:T(8,128)(2,1)S(1)}, bf16[256,512]{1,0:T(8,128)(2,1)S(1)}, u32[]{:S(2)}, u32[]{:S(2)}) %collective-permute-start.139) | collective-permute-done | bytes 262176 | tf_op jit(solution)/shard_map/ppermute | solution.py:18
  176.1 3.0 %collective-permute-start.146 = (bf16[384,512]{1,0:T(8,128)(2,1)S(1)}, bf16[384,512]{1,0:T(8,128)(2,1)S(1)}, u32[]{:S(2)}, u32[]{:S(2)}) collective-permute-start(bf16[384,512]{1,0:T(8,128)(2,1)S(1)} %get-tuple-element.329), channel_id=1, source_target_pairs={{0,248},{8,240},{16,232},{24,224},{32,216},{40,208},{48,200},{56,1... | collective-permute-start | bytes 1179656 | tf_op jit(solution)/shard_map/ppermute | solution.py:18
  179.1 0.1 collective-permute-start.145
  179.2 2.7 %collective-permute-start.144 = (bf16[256,512]{1,0:T(8,128)(2,1)S(1)}, bf16[256,512]{1,0:T(8,128)(2,1)S(1)}, u32[]{:S(2)}, u32[]{:S(2)}) collective-permute-start(bf16[256,512]{1,0:T(8,128)(2,1)S(1)} %collective-permute-done.139.refs_4_), channel_id=1, source_target_pairs={{0,2},{1,3},{2,0},{3,1},{4,6},{5,7},{6,4},{7,5},{8,10},{9,11},{10,... | collective-permute-start | bytes 786440 | tf_op jit(solution)/shard_map/ppermute | solution.py:18
  181.8 1.8 collective-permute-start.143
  183.6 11.3 %collective-permute-done.145.refs_7_ = bf16[256,512]{1,0:T(8,128)(2,1)S(1)} collective-permute-done((bf16[256,512]{1,0:T(8,128)(2,1)S(1)}, bf16[256,512]{1,0:T(8,128)(2,1)S(1)}, u32[]{:S(2)}, u32[]{:S(2)}) %collective-permute-start.145) | collective-permute-done | bytes 262176 | tf_op jit(solution)/shard_map/ppermute | solution.py:18
  194.9 1.0 collective-permute-done.143.refs_5_
  195.9 4.8 %stratum_1.1 = (bf16[256,512]{1,0:T(8,128)(2,1)S(1)}, bf16[256,512]{1,0:T(8,128)(2,1)S(1)}, bf16[256,512]{1,0:T(8,128)(2,1)S(1)}, bf16[256,512]{1,0:T(8,128)(2,1...) custom-call(s32[1]{0:T(128)} %bitcast.me, ...), custom_call_target="tpu_custom_call" | custom-call | flops 3221225472 | bytes 9437184 | tf_op jit(solution)/shard_map/stratum_1/pallas_call | solution.py:127
  200.7 1.3 collective-permute-start.147
  201.9 1.4 collective-permute-start.148
  203.4 2.1 collective-permute-start.149
  205.5 14.8 %conditional.6 = (bf16[384,512]{1,0:T(8,128)(2,1)}) conditional(s32[]{:T(128)} %bitcast.2, bf16[384,512]{1,0:T(8,128)(2,1)S(1)} %get-tuple-element.336, bf16[384,512]{1,0:T(8,128)(2,1)S(1)} %get-tuple-element.336, bf16[384,512]{1,0:T(8,128)(2,1)S(1)} %get-tuple-element.336, ...), branch_computations={%region_64.0_spmd, %region_65.0_spmd, %region_66.0_spmd, %region_6... | conditional | bytes 1572912 | solution.py:238
  205.5 14.7 %collective-permute-done.75 = bf16[384,512]{1,0:T(8,128)(2,1)} collective-permute-done((bf16[384,512]{1,0:T(8,128)(2,1)S(1)}, bf16[384,512]{1,0:T(8,128)(2,1)}, u32[]{:S(2)}, u32[]{:S(2)}) %collective-permute-start.75) | collective-permute-done | bytes 393248 | tf_op jit(solution)/shard_map/cond/branch_13_fun/ppermute | solution.py:18
  220.3 1.9 add_convert_fusion
  222.3 0.4 collective-permute-start.150
  222.7 1.9 collective-permute-start.151
  224.5 2.4 collective-permute-start.152
  227.0 5.8 %collective-permute-start.153 = (bf16[256,512]{1,0:T(8,128)(2,1)}, bf16[256,512]{1,0:T(8,128)(2,1)S(1)}, u32[]{:S(2)}, u32[]{:S(2)}) collective-permute-start(bf16[256,512]{1,0:T(8,128)(2,1)} %add_convert_fusion), channel_id=1, source_target_pairs={{0,4},{1,5},{2,6},{3,7},{4,0},{5,1},{6,2},{7,3},{8,12},{9,13},{10,... | collective-permute-start | bytes 786440 | tf_op jit(solution)/shard_map/ppermute | solution.py:18
  232.8 19.1 %conditional.7 = (bf16[640,512]{1,0:T(8,128)(2,1)}) conditional(s32[]{:T(128)} %bitcast.2, bf16[640,512]{1,0:T(8,128)(2,1)S(1)} %get-tuple-element.345, bf16[640,512]{1,0:T(8,128)(2,1)S(1)} %get-tuple-element.345, bf16[640,512]{1,0:T(8,128)(2,1)S(1)} %get-tuple-element.345, ...), branch_computations={%region_96.0_spmd, %region_97.0_spmd, %region_98.0_spmd, %region_9... | conditional | bytes 2621488 | solution.py:238
  232.8 18.9 %collective-permute-done.106 = bf16[640,512]{1,0:T(8,128)(2,1)} collective-permute-done((bf16[640,512]{1,0:T(8,128)(2,1)S(1)}, bf16[640,512]{1,0:T(8,128)(2,1)}, u32[]{:S(2)}, u32[]{:S(2)}) %collective-permute-start.106) | collective-permute-done | bytes 655392 | tf_op jit(solution)/shard_map/cond/branch_13_fun/ppermute | solution.py:18
  252.0 3.4 %finish.1 = (bf16[256,512]{1,0:T(8,128)(2,1)}, bf16[1024,512]{1,0:T(8,128)(2,1)}) custom-call(f32[2]{0:T(128)S(1)} %copy-done.2, bf16[256,512]{1,0:T(8,128)(2,1)S(1)} %get-tuple-element.330.refs_0_, bf16[256,512]{1,0:T(8,128)(2,1)S(1)} %collective-permute-done.150.refs_1_, bf16[256,512]{1,0:T(8,128)(2,1)S(1)} %collective-permute-done.151.refs_2_, ...), custom_call_target="tpu_custom_call" | custom-call | tf_op jit(solution)/shard_map/finish/pallas_call | solution.py:193
  (30 shorter events, 0.1 us)
Async XLA Ops:
  0.6 47.3 %collective-permute-start.126 = (bf16[256,512]{1,0:T(8,128)(2,1)}, bf16[256,512]{1,0:T(8,128)(2,1)S(1)}, u32[]{:S(2)}, u32[]{:S(2)}) collective-permute-start(bf16[256,512]{1,0:T(8,128)(2,1)} %refs_0_.1), channel_id=1, source_target_pairs={{0,2},{1,3},{2,0},{3,1},{4,6},{5,7},{6,4},{7,5},{8,10},{9,11},{10,... | collective-permute-start | bytes 786440 | tf_op jit(solution)/shard_map/ppermute | solution.py:18
  3.9 44.0 %collective-permute-start.125 = (bf16[256,512]{1,0:T(8,128)(2,1)}, bf16[256,512]{1,0:T(8,128)(2,1)S(1)}, u32[]{:S(2)}, u32[]{:S(2)}) collective-permute-start(bf16[256,512]{1,0:T(8,128)(2,1)} %refs_0_.1), channel_id=1, source_target_pairs={{0,1},{1,0},{2,3},{3,2},{4,5},{5,4},{6,7},{7,6},{8,9},{9,8},{10,11... | collective-permute-start | bytes 786440 | tf_op jit(solution)/shard_map/ppermute | solution.py:18
  4.6 43.4 %collective-permute-start.124 = (bf16[256,512]{1,0:T(8,128)(2,1)}, bf16[256,512]{1,0:T(8,128)(2,1)S(1)}, u32[]{:S(2)}, u32[]{:S(2)}) collective-permute-start(bf16[256,512]{1,0:T(8,128)(2,1)} %refs_0_.1), channel_id=1, source_target_pairs={{0,4},{1,5},{2,6},{3,7},{4,0},{5,1},{6,2},{7,3},{8,12},{9,13},{10,... | collective-permute-start | bytes 786440 | tf_op jit(solution)/shard_map/ppermute | solution.py:18
  10.0 38.0 %collective-permute-start.127 = (bf16[256,512]{1,0:T(8,128)(2,1)}, bf16[256,512]{1,0:T(8,128)(2,1)S(1)}, u32[]{:S(2)}, u32[]{:S(2)}) collective-permute-start(bf16[256,512]{1,0:T(8,128)(2,1)} %refs_0_.1), channel_id=1, source_target_pairs={{0,3},{1,2},{2,1},{3,0},{4,7},{5,6},{6,5},{7,4},{8,11},{9,10},{10,... | collective-permute-start | bytes 786440 | tf_op jit(solution)/shard_map/ppermute | solution.py:18
  12.2 39.9 %copy-start.5 = (s32[2,1,1]{0,2,1:T(1,128)S(1)}, s32[2,1,1]{0,2,1:T(1,128)}, u32[]{:S(2)}) copy-start(s32[2,1,1]{0,2,1:T(1,128)} %param.143) | copy-start | bytes 28
  13.3 23.6 %collective-permute-start.12 = (bf16[384,512]{1,0:T(8,128)(2,1)S(1)}, bf16[384,512]{1,0:T(8,128)(2,1)}, u32[]{:S(2)}, u32[]{:S(2)}) collective-permute-start(bf16[384,512]{1,0:T(8,128)(2,1)S(1)} %slice.147), channel_id=1, source_target_pairs={{0,104},{8,96},{16,120},{24,112},{32,72},{40,64},{48,88},{56,80},{... | collective-permute-start | bytes 1179656 | tf_op jit(solution)/shard_map/cond/branch_13_fun/ppermute | solution.py:18
  48.0 45.8 %collective-permute-start.130 = (bf16[256,512]{1,0:T(8,128)(2,1)S(1)}, bf16[256,512]{1,0:T(8,128)(2,1)S(1)}, u32[]{:S(2)}, u32[]{:S(2)}) collective-permute-start(bf16[256,512]{1,0:T(8,128)(2,1)S(1)} %collective-permute-done.124.refs_4_), channel_id=1, source_target_pairs={{0,3},{1,2},{2,1},{3,0},{4,7},{5,6},{6,5},{7,4},{8,11},{9,10},{10,... | collective-permute-start | bytes 786440 | tf_op jit(solution)/shard_map/ppermute | solution.py:18
  48.8 45.0 %collective-permute-start.129 = (bf16[256,512]{1,0:T(8,128)(2,1)S(1)}, bf16[256,512]{1,0:T(8,128)(2,1)S(1)}, u32[]{:S(2)}, u32[]{:S(2)}) collective-permute-start(bf16[256,512]{1,0:T(8,128)(2,1)S(1)} %collective-permute-done.124.refs_4_), channel_id=1, source_target_pairs={{0,2},{1,3},{2,0},{3,1},{4,6},{5,7},{6,4},{7,5},{8,10},{9,11},{10,... | collective-permute-start | bytes 786440 | tf_op jit(solution)/shard_map/ppermute | solution.py:18
  51.4 42.3 %collective-permute-start.128 = (bf16[256,512]{1,0:T(8,128)(2,1)S(1)}, bf16[256,512]{1,0:T(8,128)(2,1)S(1)}, u32[]{:S(2)}, u32[]{:S(2)}) collective-permute-start(bf16[256,512]{1,0:T(8,128)(2,1)S(1)} %collective-permute-done.124.refs_4_), channel_id=1, source_target_pairs={{0,1},{1,0},{2,3},{3,2},{4,5},{5,4},{6,7},{7,6},{8,9},{9,8},{10,11... | collective-permute-start | bytes 786440 | tf_op jit(solution)/shard_map/ppermute | solution.py:18
  52.2 41.6 %copy-start.1 = (bf16[256,512]{1,0:T(8,128)(2,1)S(1)}, bf16[256,512]{1,0:T(8,128)(2,1)}, u32[]{:S(2)}) copy-start(bf16[256,512]{1,0:T(8,128)(2,1)} %refs_0_.1) | copy-start | bytes 786436
  52.2 41.6 %copy-start.2 = (f32[2]{0:T(128)S(1)}, f32[2]{0:T(128)}, u32[]{:S(2)}) copy-start(f32[2]{0:T(128)} %step.5) | copy-start | bytes 28
  52.2 41.6 %copy-start.3 = (s32[2,1,1,16]{3,2,1,0:T(1,128)S(1)}, s32[2,1,1,16]{3,2,1,0:T(1,128)}, u32[]{:S(2)}) copy-start(s32[2,1,1,16]{3,2,1,0:T(1,128)} %row_pick.3) | copy-start | bytes 388
  52.2 41.6 %copy-start.4 = (s32[2,1,1,16]{3,2,1,0:T(1,128)S(1)}, s32[2,1,1,16]{3,2,1,0:T(1,128)}, u32[]{:S(2)}) copy-start(s32[2,1,1,16]{3,2,1,0:T(1,128)} %col_pick.3) | copy-start | bytes 388
  53.5 31.9 %collective-permute-start.43 = (bf16[640,512]{1,0:T(8,128)(2,1)S(1)}, bf16[640,512]{1,0:T(8,128)(2,1)}, u32[]{:S(2)}, u32[]{:S(2)}) collective-permute-start(bf16[640,512]{1,0:T(8,128)(2,1)S(1)} %slice.179), channel_id=1, source_target_pairs={{0,104},{8,96},{16,120},{24,112},{32,72},{40,64},{48,88},{56,80},{... | collective-permute-start | bytes 1966088 | tf_op jit(solution)/shard_map/cond/branch_13_fun/ppermute | solution.py:18
  93.8 61.0 %copy-start = (bf16[2,256,512]{2,1,0:T(8,128)(2,1)S(1)}, bf16[2,256,512]{2,1,0:T(8,128)(2,1)}, u32[]{:S(2)}) copy-start(bf16[2,256,512]{2,1,0:T(8,128)(2,1)} %refs_6_.1) | copy-start | bytes 1572868
  99.9 10.3 %collective-permute-start.131 = (bf16[256,512]{1,0:T(8,128)(2,1)S(1)}, bf16[256,512]{1,0:T(8,128)(2,1)S(1)}, u32[]{:S(2)}, u32[]{:S(2)}) collective-permute-start(bf16[256,512]{1,0:T(8,128)(2,1)S(1)} %get-tuple-element.313), channel_id=1, source_target_pairs={{0,1},{1,0},{2,3},{3,2},{4,5},{5,4},{6,7},{7,6},{8,9},{9,8},{10,11... | collective-permute-start | bytes 786440 | tf_op jit(solution)/shard_map/ppermute | solution.py:18
  103.4 10.9 %collective-permute-start.132 = (bf16[256,512]{1,0:T(8,128)(2,1)S(1)}, bf16[256,512]{1,0:T(8,128)(2,1)S(1)}, u32[]{:S(2)}, u32[]{:S(2)}) collective-permute-start(bf16[256,512]{1,0:T(8,128)(2,1)S(1)} %get-tuple-element.314), channel_id=1, source_target_pairs={{0,2},{1,3},{2,0},{3,1},{4,6},{5,7},{6,4},{7,5},{8,10},{9,11},{10,... | collective-permute-start | bytes 786440 | tf_op jit(solution)/shard_map/ppermute | solution.py:18
  103.4 13.5 %collective-permute-start.133 = (bf16[256,512]{1,0:T(8,128)(2,1)S(1)}, bf16[256,512]{1,0:T(8,128)(2,1)S(1)}, u32[]{:S(2)}, u32[]{:S(2)}) collective-permute-start(bf16[256,512]{1,0:T(8,128)(2,1)S(1)} %get-tuple-element.315), channel_id=1, source_target_pairs={{0,3},{1,2},{2,1},{3,0},{4,7},{5,6},{6,5},{7,4},{8,11},{9,10},{10,... | collective-permute-start | bytes 786440 | tf_op jit(solution)/shard_map/ppermute | solution.py:18
  106.2 48.6 %collective-permute-start.138 = (bf16[640,512]{1,0:T(8,128)(2,1)S(1)}, bf16[640,512]{1,0:T(8,128)(2,1)S(1)}, u32[]{:S(2)}, u32[]{:S(2)}) collective-permute-start(bf16[640,512]{1,0:T(8,128)(2,1)S(1)} %get-tuple-element.321), channel_id=1, source_target_pairs={{0,248},{8,240},{16,232},{24,224},{32,216},{40,208},{48,200},{56,1... | collective-permute-start | bytes 1966088 | tf_op jit(solution)/shard_map/ppermute | solution.py:18
  117.0 21.9 %collective-permute-start.137 = (bf16[256,512]{1,0:T(8,128)(2,1)S(1)}, bf16[256,512]{1,0:T(8,128)(2,1)S(1)}, u32[]{:S(2)}, u32[]{:S(2)}) collective-permute-start(bf16[256,512]{1,0:T(8,128)(2,1)S(1)} %add_convert_fusion.1), channel_id=1, source_target_pairs={{0,4},{1,5},{2,6},{3,7},{4,0},{5,1},{6,2},{7,3},{8,12},{9,13},{10,... | collective-permute-start | bytes 786440 | tf_op jit(solution)/shard_map/ppermute | solution.py:18
  120.3 34.5 %collective-permute-start.134 = (bf16[256,512]{1,0:T(8,128)(2,1)S(1)}, bf16[256,512]{1,0:T(8,128)(2,1)S(1)}, u32[]{:S(2)}, u32[]{:S(2)}) collective-permute-start(bf16[256,512]{1,0:T(8,128)(2,1)S(1)} %get-tuple-element.316), channel_id=1, source_target_pairs={{0,1},{1,0},{2,3},{3,2},{4,5},{5,4},{6,7},{7,6},{8,9},{9,8},{10,11... | collective-permute-start | bytes 786440 | tf_op jit(solution)/shard_map/ppermute | solution.py:18
  120.3 34.5 %collective-permute-start.135 = (bf16[256,512]{1,0:T(8,128)(2,1)S(1)}, bf16[256,512]{1,0:T(8,128)(2,1)S(1)}, u32[]{:S(2)}, u32[]{:S(2)}) collective-permute-start(bf16[256,512]{1,0:T(8,128)(2,1)S(1)} %get-tuple-element.318), channel_id=1, source_target_pairs={{0,2},{1,3},{2,0},{3,1},{4,6},{5,7},{6,4},{7,5},{8,10},{9,11},{10,... | collective-permute-start | bytes 786440 | tf_op jit(solution)/shard_map/ppermute | solution.py:18
  122.2 32.6 %collective-permute-start.136 = (bf16[256,512]{1,0:T(8,128)(2,1)S(1)}, bf16[256,512]{1,0:T(8,128)(2,1)S(1)}, u32[]{:S(2)}, u32[]{:S(2)}) collective-permute-start(bf16[256,512]{1,0:T(8,128)(2,1)S(1)} %get-tuple-element.320), channel_id=1, source_target_pairs={{0,3},{1,2},{2,1},{3,0},{4,7},{5,6},{6,5},{7,4},{8,11},{9,10},{10,... | collective-permute-start | bytes 786440 | tf_op jit(solution)/shard_map/ppermute | solution.py:18
  155.1 12.6 %collective-permute-start.142 = (bf16[256,512]{1,0:T(8,128)(2,1)S(1)}, bf16[256,512]{1,0:T(8,128)(2,1)S(1)}, u32[]{:S(2)}, u32[]{:S(2)}) collective-permute-start(bf16[256,512]{1,0:T(8,128)(2,1)S(1)} %fusion.2.refs_0_.refs_5_), channel_id=1, source_target_pairs={{0,3},{1,2},{2,1},{3,0},{4,7},{5,6},{6,5},{7,4},{8,11},{9,10},{10,... | collective-permute-start | bytes 786440 | tf_op jit(solution)/shard_map/ppermute | solution.py:18
  155.7 12.1 %collective-permute-start.141 = (bf16[256,512]{1,0:T(8,128)(2,1)S(1)}, bf16[256,512]{1,0:T(8,128)(2,1)S(1)}, u32[]{:S(2)}, u32[]{:S(2)}) collective-permute-start(bf16[256,512]{1,0:T(8,128)(2,1)S(1)} %fusion.2.refs_0_.refs_5_), channel_id=1, source_target_pairs={{0,2},{1,3},{2,0},{3,1},{4,6},{5,7},{6,4},{7,5},{8,10},{9,11},{10,... | collective-permute-start | bytes 786440 | tf_op jit(solution)/shard_map/ppermute | solution.py:18
  158.0 10.4 %collective-permute-start.140 = (bf16[256,512]{1,0:T(8,128)(2,1)S(1)}, bf16[256,512]{1,0:T(8,128)(2,1)S(1)}, u32[]{:S(2)}, u32[]{:S(2)}) collective-permute-start(bf16[256,512]{1,0:T(8,128)(2,1)S(1)} %fusion.2.refs_0_.refs_5_), channel_id=1, source_target_pairs={{0,1},{1,0},{2,3},{3,2},{4,5},{5,4},{6,7},{7,6},{8,9},{9,8},{10,11... | collective-permute-start | bytes 786440 | tf_op jit(solution)/shard_map/ppermute | solution.py:18
  159.3 16.8 %collective-permute-start.139 = (bf16[256,512]{1,0:T(8,128)(2,1)S(1)}, bf16[256,512]{1,0:T(8,128)(2,1)S(1)}, u32[]{:S(2)}, u32[]{:S(2)}) collective-permute-start(bf16[256,512]{1,0:T(8,128)(2,1)S(1)} %fusion.2.refs_0_.refs_5_), channel_id=1, source_target_pairs={{0,4},{1,5},{2,6},{3,7},{4,0},{5,1},{6,2},{7,3},{8,12},{9,13},{10,... | collective-permute-start | bytes 786440 | tf_op jit(solution)/shard_map/ppermute | solution.py:18
  176.1 19.8 %collective-permute-start.146 = (bf16[384,512]{1,0:T(8,128)(2,1)S(1)}, bf16[384,512]{1,0:T(8,128)(2,1)S(1)}, u32[]{:S(2)}, u32[]{:S(2)}) collective-permute-start(bf16[384,512]{1,0:T(8,128)(2,1)S(1)} %get-tuple-element.329), channel_id=1, source_target_pairs={{0,248},{8,240},{16,232},{24,224},{32,216},{40,208},{48,200},{56,1... | collective-permute-start | bytes 1179656 | tf_op jit(solution)/shard_map/ppermute | solution.py:18
  179.1 15.8 %collective-permute-start.145 = (bf16[256,512]{1,0:T(8,128)(2,1)S(1)}, bf16[256,512]{1,0:T(8,128)(2,1)S(1)}, u32[]{:S(2)}, u32[]{:S(2)}) collective-permute-start(bf16[256,512]{1,0:T(8,128)(2,1)S(1)} %collective-permute-done.139.refs_4_), channel_id=1, source_target_pairs={{0,3},{1,2},{2,1},{3,0},{4,7},{5,6},{6,5},{7,4},{8,11},{9,10},{10,... | collective-permute-start | bytes 786440 | tf_op jit(solution)/shard_map/ppermute | solution.py:18
  179.2 15.7 %collective-permute-start.144 = (bf16[256,512]{1,0:T(8,128)(2,1)S(1)}, bf16[256,512]{1,0:T(8,128)(2,1)S(1)}, u32[]{:S(2)}, u32[]{:S(2)}) collective-permute-start(bf16[256,512]{1,0:T(8,128)(2,1)S(1)} %collective-permute-done.139.refs_4_), channel_id=1, source_target_pairs={{0,2},{1,3},{2,0},{3,1},{4,6},{5,7},{6,4},{7,5},{8,10},{9,11},{10,... | collective-permute-start | bytes 786440 | tf_op jit(solution)/shard_map/ppermute | solution.py:18
  181.8 14.0 %collective-permute-start.143 = (bf16[256,512]{1,0:T(8,128)(2,1)S(1)}, bf16[256,512]{1,0:T(8,128)(2,1)S(1)}, u32[]{:S(2)}, u32[]{:S(2)}) collective-permute-start(bf16[256,512]{1,0:T(8,128)(2,1)S(1)} %collective-permute-done.139.refs_4_), channel_id=1, source_target_pairs={{0,1},{1,0},{2,3},{3,2},{4,5},{5,4},{6,7},{7,6},{8,9},{9,8},{10,11... | collective-permute-start | bytes 786440 | tf_op jit(solution)/shard_map/ppermute | solution.py:18
  200.7 19.6 %collective-permute-start.147 = (bf16[256,512]{1,0:T(8,128)(2,1)}, bf16[256,512]{1,0:T(8,128)(2,1)}, u32[]{:S(2)}, u32[]{:S(2)}) collective-permute-start(bf16[256,512]{1,0:T(8,128)(2,1)} %get-tuple-element.333), channel_id=1, source_target_pairs={{0,1},{1,0},{2,3},{3,2},{4,5},{5,4},{6,7},{7,6},{8,9},{9,8},{10,11... | collective-permute-start | bytes 786440 | tf_op jit(solution)/shard_map/ppermute | solution.py:18
  201.9 18.4 %collective-permute-start.148 = (bf16[256,512]{1,0:T(8,128)(2,1)S(1)}, bf16[256,512]{1,0:T(8,128)(2,1)}, u32[]{:S(2)}, u32[]{:S(2)}) collective-permute-start(bf16[256,512]{1,0:T(8,128)(2,1)S(1)} %get-tuple-element.334), channel_id=1, source_target_pairs={{0,2},{1,3},{2,0},{3,1},{4,6},{5,7},{6,4},{7,5},{8,10},{9,11},{10,... | collective-permute-start | bytes 786440 | tf_op jit(solution)/shard_map/ppermute | solution.py:18
  203.4 17.0 %collective-permute-start.149 = (bf16[256,512]{1,0:T(8,128)(2,1)S(1)}, bf16[256,512]{1,0:T(8,128)(2,1)}, u32[]{:S(2)}, u32[]{:S(2)}) collective-permute-start(bf16[256,512]{1,0:T(8,128)(2,1)S(1)} %get-tuple-element.335), channel_id=1, source_target_pairs={{0,3},{1,2},{2,1},{3,0},{4,7},{5,6},{6,5},{7,4},{8,11},{9,10},{10,... | collective-permute-start | bytes 786440 | tf_op jit(solution)/shard_map/ppermute | solution.py:18
  205.5 14.7 %collective-permute-start.75 = (bf16[384,512]{1,0:T(8,128)(2,1)S(1)}, bf16[384,512]{1,0:T(8,128)(2,1)}, u32[]{:S(2)}, u32[]{:S(2)}) collective-permute-start(bf16[384,512]{1,0:T(8,128)(2,1)S(1)} %param.77), channel_id=1, source_target_pairs={{0,144},{8,152},{16,128},{24,136},{32,176},{40,184},{48,160},{56,1... | collective-permute-start | bytes 1179656 | tf_op jit(solution)/shard_map/cond/branch_13_fun/ppermute | solution.py:18
  222.3 29.6 %collective-permute-start.150 = (bf16[256,512]{1,0:T(8,128)(2,1)S(1)}, bf16[256,512]{1,0:T(8,128)(2,1)S(1)}, u32[]{:S(2)}, u32[]{:S(2)}) collective-permute-start(bf16[256,512]{1,0:T(8,128)(2,1)S(1)} %get-tuple-element.338), channel_id=1, source_target_pairs={{0,1},{1,0},{2,3},{3,2},{4,5},{5,4},{6,7},{7,6},{8,9},{9,8},{10,11... | collective-permute-start | bytes 786440 | tf_op jit(solution)/shard_map/ppermute | solution.py:18
  222.7 29.3 %collective-permute-start.151 = (bf16[256,512]{1,0:T(8,128)(2,1)S(1)}, bf16[256,512]{1,0:T(8,128)(2,1)S(1)}, u32[]{:S(2)}, u32[]{:S(2)}) collective-permute-start(bf16[256,512]{1,0:T(8,128)(2,1)S(1)} %get-tuple-element.340), channel_id=1, source_target_pairs={{0,2},{1,3},{2,0},{3,1},{4,6},{5,7},{6,4},{7,5},{8,10},{9,11},{10,... | collective-permute-start | bytes 786440 | tf_op jit(solution)/shard_map/ppermute | solution.py:18
  224.5 27.4 %collective-permute-start.152 = (bf16[256,512]{1,0:T(8,128)(2,1)S(1)}, bf16[256,512]{1,0:T(8,128)(2,1)S(1)}, u32[]{:S(2)}, u32[]{:S(2)}) collective-permute-start(bf16[256,512]{1,0:T(8,128)(2,1)S(1)} %get-tuple-element.342), channel_id=1, source_target_pairs={{0,3},{1,2},{2,1},{3,0},{4,7},{5,6},{6,5},{7,4},{8,11},{9,10},{10,... | collective-permute-start | bytes 786440 | tf_op jit(solution)/shard_map/ppermute | solution.py:18
  227.0 25.0 %collective-permute-start.153 = (bf16[256,512]{1,0:T(8,128)(2,1)}, bf16[256,512]{1,0:T(8,128)(2,1)S(1)}, u32[]{:S(2)}, u32[]{:S(2)}) collective-permute-start(bf16[256,512]{1,0:T(8,128)(2,1)} %add_convert_fusion), channel_id=1, source_target_pairs={{0,4},{1,5},{2,6},{3,7},{4,0},{5,1},{6,2},{7,3},{8,12},{9,13},{10,... | collective-permute-start | bytes 786440 | tf_op jit(solution)/shard_map/ppermute | solution.py:18
  232.8 18.9 %collective-permute-start.106 = (bf16[640,512]{1,0:T(8,128)(2,1)S(1)}, bf16[640,512]{1,0:T(8,128)(2,1)}, u32[]{:S(2)}, u32[]{:S(2)}) collective-permute-start(bf16[640,512]{1,0:T(8,128)(2,1)S(1)} %param.109), channel_id=1, source_target_pairs={{0,144},{8,152},{16,128},{24,136},{32,176},{40,184},{48,160},{56,1... | collective-permute-start | bytes 1966088 | tf_op jit(solution)/shard_map/cond/branch_13_fun/ppermute | solution.py:18
